TPU v7x, 256 devices: a whole 4x4x8 slice. The times are simulated.
256 devices in a mesh: dp: 16 (over y, x), proto: 16 (over z, core).
Axes of the slice: x: 4, y: 4, z: 8, core: 2. Of those that a mesh axis runs over, the one named last changes fastest.
Arguments:
- teacher_feats: bfloat16 [4096, 256], P('dp', 'proto'), may hold values from -8 to 8
- student_feats: bfloat16 [4096, 256], P('dp', 'proto'), may hold values from -6 to 6
- prototypes: bfloat16 [256, 131072], P('dp', 'proto'), may hold values from -0.5 to 0.5
Outputs:
- loss: float32 [], replicated
- grad_proto: float32 [256, 131072], P('dp', 'proto')
- grad_student: float32 [4096, 256], P('dp', 'proto')
All inputs are finite; a program needn't handle non-finite values.
Results may differ from a plain program's by a relative error of at most 0.00045.
The roundings to bfloat16 on the way count: a program that leaves them out, or rounds other values in their place, can miss the bound.
Values may be sent and summed in bfloat16 or wider, within the bound.
A program may use at most 64 MiB of HBM per device.

v0:
```python
import jax
import jax.numpy as jnp
from jax import lax
from jax.sharding import PartitionSpec as P

ITERS = 3


eps = 1e-06
teacher_temp = 0.07
student_temp = 0.1


def row_totals(base, col_scale):
    local = jnp.dot(base, col_scale, precision=lax.Precision.HIGHEST)
    return lax.psum(local, "proto")


def col_totals(row_scale, base):
    local = jnp.dot(row_scale, base, precision=lax.Precision.HIGHEST)
    return lax.psum(local, "dp")


def body(teacher_feats, student_feats, prototypes):
    teacher_full, student_full = (
        lax.all_gather(teacher_feats, "proto", axis=1, tiled=True),
        lax.all_gather(student_feats, "proto", axis=1, tiled=True),
    )
    t32 = teacher_full.astype(jnp.float32)
    t_unit = (t32 * lax.rsqrt(jnp.sum(t32 * t32, axis=1, keepdims=True) + eps)).astype(jnp.bfloat16)
    s32 = student_full.astype(jnp.float32)
    s_inv = lax.rsqrt(jnp.sum(s32 * s32, axis=1, keepdims=True) + eps)
    s_unit32 = s32 * s_inv
    s_unit = s_unit32.astype(jnp.bfloat16)
    columns = lax.all_gather(prototypes, "dp", axis=0, tiled=True)
    w32 = columns.astype(jnp.float32)
    w_inv = lax.rsqrt(jnp.sum(w32 * w32, axis=0, keepdims=True) + eps)
    w_unit32 = w32 * w_inv
    w_unit = w_unit32.astype(jnp.bfloat16)
    row_count = teacher_full.shape[0]
    all_rows = row_count * lax.axis_size("dp")
    all_protos = columns.shape[1] * lax.axis_size("proto")
    loss_scale = all_rows * all_protos // 256
    factor = float(loss_scale) / float(all_rows) / student_temp
    base = jnp.exp(jnp.dot(t_unit, w_unit, preferred_element_type=jnp.float32) / teacher_temp)
    logits = jnp.dot(s_unit, w_unit, preferred_element_type=jnp.float32) / student_temp
    expo = jnp.exp(logits)
    totals = lax.psum(jnp.sum(expo, axis=1), "proto")
    row_scale = jnp.ones((row_count,), jnp.float32)
    for step in range(ITERS - 1):
        col_scale = 1.0 / col_totals(row_scale, base)
        row_scale = 1.0 / row_totals(base, col_scale)
    col_scale = 1.0 / col_totals(row_scale, base)
    row_scale = 1.0 / row_totals(base, col_scale)
    targets = base * row_scale[:, None] * col_scale[None, :]
    log_total = jnp.log(totals)[:, None]
    local_loss = jnp.sum(targets * (logits - log_total))
    loss = -lax.psum(local_loss, ("dp", "proto")) / float(all_rows)
    grad_logits = ((expo / totals[:, None] - targets) * factor).astype(jnp.bfloat16)
    grad_wunit = lax.dot_general(
        s_unit, grad_logits, (((0,), (0,)), ((), ())), preferred_element_type=jnp.float32
    )
    grad_sunit = lax.dot_general(
        grad_logits, w_unit, (((1,), (1,)), ((), ())), preferred_element_type=jnp.float32
    )
    summed_w = lax.psum_scatter(grad_wunit, "dp", scatter_dimension=0, tiled=True)
    width_w = summed_w.shape[0]
    own_w = lax.dynamic_slice_in_dim(w_unit32, lax.axis_index("dp") * width_w, width_w, 0)
    col_dots = lax.psum(jnp.sum(own_w * summed_w, axis=0), "dp")
    grad_proto = w_inv * (summed_w - own_w * col_dots[None, :])
    summed_s = lax.psum_scatter(grad_sunit, "proto", scatter_dimension=1, tiled=True)
    width_s = summed_s.shape[1]
    own_s = lax.dynamic_slice_in_dim(s_unit32, lax.axis_index("proto") * width_s, width_s, 1)
    row_dots = lax.psum(jnp.sum(own_s * summed_s, axis=1), "proto")
    grad_student = s_inv * (summed_s - own_s * row_dots[:, None])
    return (loss, grad_proto, grad_student)


def solution(mesh):
    in_specs = (P("dp", "proto"), P("dp", "proto"), P("dp", "proto"))
    out_specs = (P(), P("dp", "proto"), P("dp", "proto"))
    return jax.shard_map(body, mesh=mesh, in_specs=in_specs, out_specs=out_specs, check_vma=False)
```

profile of v0, /device:TPU:8, one launch (start us, length us, event | category | flops | bytes accessed | tf_op | source)
XLA Modules:
  0.0 649.4 jit_solution(3647295388966337998)
XLA Ops:
  7.9 20.6 %all_gather.9 = bf16[256,256]{0,1:T(8,128)(2,1)S(1)} all-gather(bf16[256,16]{0,1:T(8,128)(2,1)} %param.3), channel_id=1, replica_groups=mesh['dp'=16,'proto'=16] {'proto'}, dimensions={1}, use_global_device_ids=true | all-gather | bytes 139264 | tf_op jit(solution)/shard_map/all_gather | solution.py:26
  28.5 15.0 %all_gather.11 = bf16[256,256]{0,1:T(8,128)(2,1)S(1)} all-gather(bf16[256,16]{0,1:T(8,128)(2,1)} %param.4), channel_id=1, replica_groups=mesh['dp'=16,'proto'=16] {'proto'}, dimensions={1}, use_global_device_ids=true | all-gather | bytes 139264 | tf_op jit(solution)/shard_map/all_gather | solution.py:27
  43.7 26.1 %all-gather.2.cloned.1.call-done = bf16[256,8192]{1,0:T(8,128)(2,1)} async-done(((bf16[16,8192]{1,0:T(8,128)(2,1)}), bf16[256,8192]{1,0:T(8,128)(2,1)}) %all-gather.2.cloned.1.call-update) | async-done | bytes 4194320 | tf_op jit(solution)/shard_map/all_gather | solution.py:35
  69.8 3.1 fusion.1
  72.9 4.2 fusion
  77.1 3.2 copy-done
  80.3 4.0 fusion.15
  84.3 66.4 %psum.70 = f32[8192]{0:T(1024)S(1)} all-reduce(f32[8192]{0:T(1024)S(1)} %bitcast.29), channel_id=1, replica_groups=mesh['dp'=16,'proto'=16] {'dp'}, use_global_device_ids=true, to_apply=%region_2.0 | all-reduce | flops 8192 | bytes 65536 | tf_op jit(solution)/shard_map/psum | solution.py:21
  150.7 8.9 %fusion.18 = f32[1,256]{1,0:T(1,128)S(1)} fusion(f32[256,8192]{1,0:T(8,128)} %copy-done, f32[8192,1]{0,1:T(1,128)S(1)} %bitcast.25), kind=kOutput, calls=%fused_computation.39 | convolution fusion | flops 25165824 | bytes 8422400 | tf_op jit(solution)/shard_map/dot_general | solution.py:15
  159.6 23.7 %psum.71 = f32[256]{0:T(256)S(1)} all-reduce(f32[256]{0:T(256)S(1)} %bitcast.31), channel_id=1, replica_groups=mesh['dp'=16,'proto'=16] {'proto'}, use_global_device_ids=true, to_apply=%region_3.0 | all-reduce | flops 256 | bytes 2048 | tf_op jit(solution)/shard_map/psum | solution.py:16
  183.3 7.4 %fusion.19 = f32[1,8192]{1,0:T(1,128)S(1)} fusion(f32[256,1]{0,1:T(1,128)S(1)} %bitcast.32, f32[256,8192]{1,0:T(8,128)} %copy-done), kind=kOutput, calls=%fused_computation.40 | convolution fusion | flops 25165824 | bytes 8422400 | tf_op jit(solution)/shard_map/dot_general | solution.py:20
  190.7 69.5 %psum.72 = f32[8192]{0:T(1024)S(1)} all-reduce(f32[8192]{0:T(1024)S(1)} %bitcast.26), channel_id=1, replica_groups=mesh['dp'=16,'proto'=16] {'dp'}, use_global_device_ids=true, to_apply=%region_4.0 | all-reduce | flops 8192 | bytes 65536 | tf_op jit(solution)/shard_map/psum | solution.py:21
  260.3 8.9 %fusion.20 = f32[1,256]{1,0:T(1,128)S(1)} fusion(f32[256,8192]{1,0:T(8,128)} %copy-done, f32[8192,1]{0,1:T(1,128)S(1)} %bitcast.27), kind=kOutput, calls=%fused_computation.41 | convolution fusion | flops 25165824 | bytes 8422400 | tf_op jit(solution)/shard_map/dot_general | solution.py:15
  269.2 23.5 %psum.73 = f32[256]{0:T(256)S(1)} all-reduce(f32[256]{0:T(256)S(1)} %bitcast.33), channel_id=1, replica_groups=mesh['dp'=16,'proto'=16] {'proto'}, use_global_device_ids=true, to_apply=%region_5.0 | all-reduce | flops 256 | bytes 2048 | tf_op jit(solution)/shard_map/psum | solution.py:16
  292.7 7.4 %fusion.21 = f32[1,8192]{1,0:T(1,128)S(1)} fusion(f32[256,1]{0,1:T(1,128)S(1)} %bitcast.34, f32[256,8192]{1,0:T(8,128)} %copy-done), kind=kOutput, calls=%fused_computation.42 | convolution fusion | flops 25165824 | bytes 8422400 | tf_op jit(solution)/shard_map/dot_general | solution.py:20
  300.1 69.8 %psum.74 = f32[8192]{0:T(1024)S(1)} all-reduce(f32[8192]{0:T(1024)S(1)} %bitcast.28), channel_id=1, replica_groups=mesh['dp'=16,'proto'=16] {'dp'}, use_global_device_ids=true, to_apply=%region_6.0 | all-reduce | flops 8192 | bytes 65536 | tf_op jit(solution)/shard_map/psum | solution.py:21
  369.9 9.0 %fusion.22 = f32[1,256]{1,0:T(1,128)S(1)} fusion(f32[256,8192]{1,0:T(8,128)} %copy-done, f32[8192,1]{0,1:T(1,128)S(1)} %bitcast.24), kind=kOutput, calls=%fused_computation.43 | convolution fusion | flops 25165824 | bytes 8422400 | tf_op jit(solution)/shard_map/dot_general | solution.py:15
  379.0 5.4 exponential_reduce_fusion
  384.4 23.5 %all-reduce = (f32[256]{0:T(256)S(1)}, f32[256]{0:T(256)S(1)}) all-reduce(f32[256]{0:T(256)S(1)} %get-tuple-element.7, f32[256]{0:T(256)S(1)} %bitcast.30), channel_id=1, replica_groups=mesh['dp'=16,'proto'=16] {'proto'}, use_global_device_ids=true, to_apply=%region_10.0 | all-reduce | flops 512 | bytes 4096 | tf_op jit(solution)/shard_map/psum | solution.py:48
  407.9 8.4 %multiply_convert_fusion = (bf16[256,8192]{1,0:T(8,128)(2,1)S(1)}, f32[]{:T(128)}) fusion(f32[256,8192]{1,0:T(8,128)} %get-tuple-element.8, f32[256,8192]{1,0:T(8,128)} %copy-done, f32[256]{0:T(256)S(1)} %get-tuple-element.3, f32[8192]{0:T(1024)S(1)} %broadcast_divide_fusion, f32[256]{0:T(256)S(1)} %broadcast_divide_fusion.5, f32[256]{0:T(256)S(1)} %log.3), kind=kLoop, calls=%fused_computation.6 | loop fusion | flops 18874368 | bytes 21007364 | tf_op jit(solution)/shard_map/convert_element_type | solution.py:59
  416.3 2.0 copy-done.3
  418.3 2.0 fusion.3
  420.4 6.7 %fusion.12 = f32[256,8192]{1,0:T(8,128)} fusion(bf16[256,8192]{1,0:T(8,128)(2,1)} %copy-done.3, bf16[256,256]{0,1:T(8,128)(2,1)S(1)} %all_gather.11, f32[256]{0:T(256)S(1)} %add_rsqrt_fusion.1), kind=kOutput, calls=%fused_computation.22 | convolution fusion | flops 1073938432 | bytes 12715008 | tf_op jit(solution)/shard_map/dot_general | solution.py:60
  427.1 79.1 %psum.77 = f32[]{:T(128)} all-reduce(f32[]{:T(128)} %get-tuple-element.6), channel_id=1, replica_groups=mesh['dp'=16,'proto'=16] {'dp','proto'}, use_global_device_ids=true, to_apply=%region_12.0 | all-reduce | flops 1 | bytes 8 | tf_op jit(solution)/shard_map/psum | solution.py:58
  506.9 6.6 %convert_multiply_fusion = f32[256,8192]{1,0:T(8,128)} fusion(bf16[256,8192]{1,0:T(8,128)(2,1)} %all-gather.2.cloned.1.call-done, f32[8192]{0:T(1024)S(1)} %add_rsqrt_fusion), kind=kLoop, calls=%fused_computation.3 | loop fusion | flops 4194304 | bytes 12615680 | tf_op jit(solution)/shard_map/mul | solution.py:38
  513.5 0.7 multiply_reduce_fusion.2
  514.3 27.5 %psum.79 = f32[256]{0:T(256)S(1)} all-reduce(f32[256]{0:T(256)S(1)} %multiply_reduce_fusion.2), channel_id=1, replica_groups=mesh['dp'=16,'proto'=16] {'proto'}, use_global_device_ids=true, to_apply=%region_18.0 | all-reduce | flops 256 | bytes 2048 | tf_op jit(solution)/shard_map/psum | solution.py:74
  541.8 1.3 subtract_multiply_fusion.1
  543.1 29.0 %reduce-scatter.3.cloned.1.call-done = f32[16,8192]{1,0:T(8,128)} async-done(((f32[256,8192]{1,0:T(8,128)}), f32[16,8192]{1,0:T(8,128)}) %reduce-scatter.3.cloned.1.call-update) | async-done | bytes 524304 | tf_op jit(solution)/shard_map/reduce_scatter | solution.py:66
  572.1 1.3 multiply_reduce_fusion.1
  573.4 66.3 %psum.78 = f32[8192]{0:T(1024)S(1)} all-reduce(f32[8192]{0:T(1024)S(1)} %multiply_reduce_fusion.1), channel_id=1, replica_groups=mesh['dp'=16,'proto'=16] {'dp'}, use_global_device_ids=true, to_apply=%region_15.0 | all-reduce | flops 8192 | bytes 65536 | tf_op jit(solution)/shard_map/psum | solution.py:69
  639.7 2.1 subtract_multiply_fusion
  (26 shorter events, 1.1 us)
Async XLA Ops:
  7.2 62.7 %all-gather.2.cloned.1.call-start = ((), (), s32[]{:S(2)}) async-start(), calls=%async_computation.2 | async-start | bytes 4456448 | tf_op jit(solution)/shard_map/all_gather | solution.py:35
  7.9 505.6 %reduce-scatter.5.cloned.1.call-start = ((), (), s32[]{:S(2)}) async-start(), calls=%async_computation.4 | async-start | bytes 278528 | tf_op jit(solution)/shard_map/reduce_scatter | solution.py:71
  77.1 3.2 copy-start
  369.9 9.1 %copy-start.1 = (bf16[256,8192]{1,0:T(8,128)(2,1)S(1)}, bf16[256,8192]{1,0:T(8,128)(2,1)}, u32[]{:S(2)}) copy-start(bf16[256,8192]{1,0:T(8,128)(2,1)} %all-gather.2.cloned.1.call-done) | copy-start | bytes 12582916
  407.9 10.4 %copy-start.2 = (bf16[256,8192]{1,0:T(8,128)(2,1)S(1)}, bf16[256,8192]{1,0:T(8,128)(2,1)}, u32[]{:S(2)}) copy-start(bf16[256,8192]{1,0:T(8,128)(2,1)} %all-gather.2.cloned.1.call-done) | copy-start | bytes 12582916
  416.3 2.0 copy-start.3
  420.3 151.8 %reduce-scatter.3.cloned.1.call-start = ((), (), s32[]{:S(2)}) async-start(), calls=%async_computation.3 | async-start | bytes 8912896 | tf_op jit(solution)/shard_map/reduce_scatter | solution.py:66
Sparse Core Ops, SparseCore 0:
  10.4 59.3 all-gather.1
  420.5 58.8 reduce-scatter.4
  483.5 88.5 reduce-scatter.2
where the time goes:
time: 656 us; the launch traced here: 649 us
  blocking collectives  485 us (74%)
  matrix products  63.9 us (10%)
  waiting for transfers between devices  55.9 us (9%)
  other arithmetic  23.7 us (4%)
  between operations  15.6 us (2%)
    psum x3, blocking collectives, col_totals(): return lax.psum(local, 'dp')  206 us
    psum x1, blocking collectives, body(): loss = -lax.psum(local_loss, ('dp', 'proto')) / float(all_rows)  79.1 us
    psum x1, blocking collectives, body(): col_dots = lax.psum(jnp.sum(own_w * summed_w, axis=0), 'dp')  66.3 us
    psum x2, blocking collectives, row_totals(): return lax.psum(local, 'proto')  47.3 us
    reduce_scatter x1, waiting for transfers between devices, body(): lax.psum_scatter(grad_wunit, 'dp', scatter_dimension=0, tiled=True)  29 us
    psum x1, blocking collectives, body(): row_dots = lax.psum(jnp.sum(own_s * summed_s, axis=1), 'proto')  27.5 us
    dot_general x3, matrix products, row_totals(): local = jnp.dot(base, col_scale, precision=lax.Precision.HIGHEST)  26.8 us
    all_gather x1, waiting for transfers between devices, body(): columns = lax.all_gather(prototypes, 'dp', axis=0, tiled=True)  26.1 us
  transfers between devices with their start and end apart: 3, of which 2 were waited for; matrix products, arithmetic and copies ran while one was open for 2% of the time, Pallas kernels for 0%

commit v1 on v0

v1 whole, which is shorter than its diff:
```python
import functools

import jax
import jax.numpy as jnp
from jax import lax
from jax.experimental import pallas as pl
from jax.experimental.pallas import tpu as pltpu
from jax.sharding import PartitionSpec as P

ITERS = 3
EPS = 1e-06
TEACHER_TEMP = 0.07
STUDENT_TEMP = 0.1
MESH = pl.DeviceIdType.MESH
F32 = jnp.float32
BF16 = jnp.bfloat16


def rcopy(src, dst, send_sem, recv_sem, dev):
    return pltpu.make_async_remote_copy(
        src_ref=src, dst_ref=dst, send_sem=send_sem, recv_sem=recv_sem,
        device_id=dev, device_id_type=MESH,
    )


def each(lo, hi, fn):
    def step(k, carry):
        fn(k)
        return carry
    lax.fori_loop(lo, hi, step, 0)


def dot(a, b, dims=((1,), (0,))):
    return lax.dot_general(a, b, (dims, ((), ())), preferred_element_type=F32)


def kernel(
    cfg, x_ref, w_ref, loss_ref, gp_ref, gs_ref,
    feats, wraw, wn, wtn, sn, base, logit, acc, colb, rscale, tots, gbuf, lossv,
    core_col, plane_row, z_row, gw, gw_in, gp_all,
    part_a, part_b, in_a, in_b, sum_a, sum_b, in_a2, in_b2, msg, msg_in, plane_loss,
    f_send, f_recv, w_send, w_recv, wc_sem, t_send, t_recv, s_send, s_recv,
    cc_send, cc_recv, pr_send, pr_recv, zr_send, zr_recv, gw_sem, gp_send, gp_recv,
    a_send, a_recv, b_send, b_recv, a2_send, a2_recv, b2_send, b2_recv,
    m_send, m_recv, l_send, l_recv,
):
    NP, NJ, NY, NX, factor, inv_rows = cfg
    NZ = NJ // 2
    DB = x_ref.shape[1]
    SH = x_ref.shape[2] // 2
    CB = wraw.shape[2]
    D = DB * NJ
    DH = D // 2
    PC = 2 * CB
    CH = min(256, CB)
    HX = NX // 2
    p = lax.axis_index("dp")
    j = lax.axis_index("proto")
    y, x = p // NX, lax.rem(p, NX)
    z, c = j // 2, lax.rem(j, 2)
    oc = 1 - c
    peer = (p, 2 * z + oc)

    def dp_of(yy, xx):
        return yy * NX + xx

    def nxt(v, k, n):
        return lax.rem(v + k, n)

    barrier = pltpu.get_barrier_semaphore()

    def greet_dp(k):
        pl.semaphore_signal(barrier, inc=1, device_id=(nxt(p, k, NP), j), device_id_type=MESH)

    def greet_proto(k):
        pl.semaphore_signal(barrier, inc=1, device_id=(p, nxt(j, k, NJ)), device_id_type=MESH)

    each(1, NP, greet_dp)
    each(1, NJ, greet_proto)
    pl.semaphore_wait(barrier, NP + NJ - 2)

    def half(cc):
        return x_ref.at[:, :, pl.ds(pl.multiple_of(cc * SH, SH), SH)]

    my_rows = pl.ds(pl.multiple_of(j * DB, DB), DB)

    def feat_copy(k):
        q = nxt(j, k, NJ)
        return rcopy(half(lax.rem(q, 2)), feats.at[:, y, x, my_rows], f_send.at[q], f_recv.at[j], (p, q))

    each(1, NJ, lambda k: feat_copy(k).start())

    w_rows = pl.ds(pl.multiple_of(p * DB, DB), DB)

    def w_copy(k):
        q = nxt(p, k, NP)
        cols = pl.ds(pl.multiple_of(q * CB, CB), CB)
        return rcopy(w_ref.at[:, cols], wraw.at[c, w_rows], w_send.at[q], w_recv.at[p], (q, j))

    each(1, NP, lambda k: w_copy(k).start())
    feats[:, y, x, my_rows, :] = x_ref[:, :, pl.ds(pl.multiple_of(c * SH, SH), SH)]
    wraw[c, w_rows, :] = w_ref[:, pl.ds(pl.multiple_of(p * CB, CB), CB)]

    def feat_wait(k):
        q = nxt(j, k, NJ)
        rows = pl.ds(pl.multiple_of(q * DB, DB), DB)
        rcopy(half(0), feats.at[:, y, x, rows], f_send.at[q], f_recv.at[q], (p, q)).wait_recv()

    each(1, NJ, feat_wait)

    def t_copy(xs, n, dev):
        slot = feats.at[0, y, xs]
        return rcopy(slot, slot, t_send.at[n], t_recv.at[y, xs], dev)

    def s_copy(ys, n, dev):
        slot = feats.at[1, ys, x]
        return rcopy(slot, slot, s_send.at[n], s_recv.at[ys, x], dev)

    def t_wait(yy, xx):
        slot = feats.at[0, yy, xx]
        rcopy(slot, slot, t_send.at[0], t_recv.at[yy, xx], peer).wait_recv()

    def s_wait(yy, xx):
        slot = feats.at[1, yy, xx]
        rcopy(slot, slot, s_send.at[0], s_recv.at[yy, xx], peer).wait_recv()

    def own_out(k):
        xq, yq = nxt(x, k, NX), nxt(y, k, NY)
        t_copy(x, k - 1, (dp_of(y, xq), j)).start()
        s_copy(y, k - 1, (dp_of(yq, x), j)).start()
        t_copy(x, NX - 2 + k, (dp_of(yq, x), j)).start()
        s_copy(y, NY - 2 + k, (dp_of(y, xq), j)).start()

    each(1, NX, own_out)

    def w_wait(k):
        q = nxt(p, k, NP)
        rows = pl.ds(pl.multiple_of(q * DB, DB), DB)
        rcopy(w_ref.at[:, pl.ds(0, CB)], wraw.at[c, rows], w_send.at[q], w_recv.at[q], (q, j)).wait_recv()

    each(1, NP, w_wait)
    w_core = rcopy(wraw.at[c], wraw.at[c], wc_sem.at[0], wc_sem.at[1], peer)
    w_core.start()

    def forward(k):
        xs, ys = nxt(x, k, NX), nxt(y, k, NY)
        t_wait(y, xs)
        n0 = 2 * (NX - 1) + (k - 1) * (NX - 1) - 1

        def fwd_t(m):
            t_copy(xs, n0 + m, (dp_of(nxt(y, m, NY), x), j)).start()

        each(1, NY, fwd_t)
        s_wait(ys, x)

        def fwd_s(m):
            s_copy(ys, n0 + m, (dp_of(y, nxt(x, m, NX)), j)).start()

        each(1, NX, fwd_s)

    each(1, NX, forward)

    def unit_cols(v):
        v32 = v.astype(F32)
        inv = lax.rsqrt(jnp.sum(v32 * v32, axis=0, keepdims=True) + EPS)
        return v32 * inv, inv

    def w_norm(cc):
        for h in range(CB // CH):
            u, _ = unit_cols(wraw[cc, :, h * CH:(h + 1) * CH])
            wn[cc, :, h * CH:(h + 1) * CH] = u.astype(BF16)
            wtn[cc, h * CH:(h + 1) * CH, :] = u.T.astype(BF16)

    w_norm(c)
    w_core.wait_recv()
    w_norm(oc)

    chunks = [(cc, h) for cc in range(2) for h in range(CB // CH)]

    def two(a):
        return jnp.concatenate([a, a], axis=1)

    acc[...] = jnp.zeros_like(acc)

    def teacher_rows(k):
        yy = nxt(y, k, NY)

        @pl.when(k > 0)
        def _():
            each(0, NX, lambda xx: t_wait(yy, xx))

        def pair(xp):
            b = yy * HX + xp
            raw = jnp.concatenate([feats[0, yy, 2 * xp], feats[0, yy, 2 * xp + 1]], axis=1)
            u, _ = unit_cols(raw)
            tn = u.astype(BF16)
            for i, (cc, h) in enumerate(chunks):
                rows = slice(i * CH, (i + 1) * CH)
                e = jnp.exp(dot(wtn[cc, h * CH:(h + 1) * CH, :], tn) * (1.0 / TEACHER_TEMP))
                base[b, rows, :] = e
                acc[rows, :] += e[:, :SH] + e[:, SH:]

        each(0, HX, pair)

    each(0, NY, teacher_rows)

    def student_rows(k):
        yy = nxt(y, k, NY)

        def pair(xp):
            b = yy * HX + xp

            def arrive(xx):
                @pl.when(jnp.logical_and(k >= 0, xx != x))
                def _():
                    s_wait(yy, xx)

            arrive(2 * xp)
            arrive(2 * xp + 1)
            raw = jnp.concatenate([feats[1, yy, 2 * xp], feats[1, yy, 2 * xp + 1]], axis=1)
            u, _ = unit_cols(raw)
            un = u.astype(BF16)
            sn[b] = un
            part = jnp.zeros((8, 2 * SH), F32)
            for i, (cc, h) in enumerate(chunks):
                rows = slice(i * CH, (i + 1) * CH)
                v = dot(wtn[cc, h * CH:(h + 1) * CH, :], un) * (1.0 / STUDENT_TEMP)
                logit[b, rows, :] = v
                part = part + jnp.sum(jnp.exp(v).reshape(CH // 8, 8, 2 * SH), axis=0)
            tot = jnp.sum(part, axis=0, keepdims=True)
            q = yy * NX + 2 * xp
            tots[pl.ds(q, 1), :] = tot[:, :SH]
            tots[pl.ds(q + 1, 1), :] = tot[:, SH:]

        each(0, HX, pair)

    def col_exchange(r):
        for i in range(PC // 128):
            core_col[r, c, :, i * 128:(i + 1) * 128] = jnp.sum(
                acc[i * 128:(i + 1) * 128, :].T, axis=0, keepdims=True)
        cp = rcopy(core_col.at[r, c], core_col.at[r, c], cc_send.at[r], cc_recv.at[r], peer)
        cp.start()
        cp.wait_recv()
        for i in range(PC // 128):
            s = slice(i * 128, (i + 1) * 128)
            v = 1.0 / (core_col[r, 0, :, s] + core_col[r, 1, :, s])
            colb[s, :] = jnp.broadcast_to(v, (128, 128)).T

    def col_pass():
        scale = rscale[...]

        def block(i):
            rows = pl.ds(pl.multiple_of(i * 64, 64), 64)
            a = jnp.zeros((64, SH), F32)
            for b in range(NP // 2):
                for h in range(2):
                    a = a + base[b, rows, h * SH:(h + 1) * SH] * scale[2 * b + h:2 * b + h + 1, :]
            acc[rows, :] = a

        each(0, PC // 64, block)

    def row_pass(r):
        def pair(b):
            for h in range(2):
                a = jnp.zeros((8, SH), F32)
                for i in range(PC // 64):
                    rows = slice(i * 64, (i + 1) * 64)
                    v = base[b, rows, h * SH:(h + 1) * SH] * colb[rows, :]
                    a = a + jnp.sum(v.reshape(8, 8, SH), axis=0)
                plane_row[r, p, pl.ds(2 * b + h, 1), :] = jnp.sum(a, axis=0, keepdims=True)

        each(0, NP // 2, pair)

    def row_exchange(r, between=None):
        n = 2 * NP if r == 1 else NP
        if r == 1:
            plane_row[r, p, NP:, :] = tots[...]

        def plane_copy(q, src):
            slot = plane_row.at[r, src, pl.ds(0, n)]
            return rcopy(slot, slot, pr_send.at[r, q], pr_recv.at[r, src], (q, j))

        each(1, NP, lambda k: plane_copy(nxt(p, k, NP), p).start())
        if between is not None:
            between()

        def plane_wait(k):
            q = nxt(p, k, NP)
            plane_copy(q, q).wait_recv()

        each(1, NP, plane_wait)
        total = plane_row[r, 0, :n, :]
        for q in range(1, NP):
            total = total + plane_row[r, q, :n, :]
        z_row[r, z, :n, :] = total

        def z_copy(q, src):
            slot = z_row.at[r, src, pl.ds(0, n)]
            return rcopy(slot, slot, zr_send.at[r, q], zr_recv.at[r, src], (p, 2 * q + c))

        each(1, NZ, lambda k: z_copy(nxt(z, k, NZ), z).start())

        def z_wait(k):
            q = nxt(z, k, NZ)
            z_copy(q, q).wait_recv()

        each(1, NZ, z_wait)
        total = z_row[r, 0, :n, :]
        for q in range(1, NZ):
            total = total + z_row[r, q, :n, :]
        rscale[...] = 1.0 / total[:NP]
        if r == 1:
            tots[...] = total[NP:]

    for r in range(ITERS):
        if r > 0:
            col_pass()
        col_exchange(r)
        row_pass(r)
        row_exchange(r, (lambda: each(0, NY, student_rows)) if r == 0 else None)

    lossv[...] = jnp.zeros_like(lossv)
    gw[...] = jnp.zeros_like(gw)

    def row_of(ref, q):
        return jnp.concatenate([ref[pl.ds(q, 1), :], ref[pl.ds(q + 1, 1), :]], axis=1)

    def a_copy(yy, xp, src_y):
        xs = pl.ds(2 * xp, 2)
        n = yy * HX + xp
        m = src_y * HX + xp
        return rcopy(part_a.at[yy, xs], in_a.at[src_y, xs], a_send.at[n], a_recv.at[m], (dp_of(yy, x), j))

    def b_copy(xx, yy, src_x):
        return rcopy(part_b.at[xx, yy], in_b.at[src_x, yy], b_send.at[xx, yy], b_recv.at[src_x, yy], (dp_of(y, xx), j))

    def grad_rows(k):
        yy = nxt(y, k + 1, NY)

        def pair(xp):
            b = yy * HX + xp
            q = yy * NX + 2 * xp
            rs = row_of(rscale, q)
            tot = row_of(tots, q)
            inv_tot = 1.0 / tot
            log_tot = jnp.log(tot)
            lsum = jnp.zeros((8, 2 * SH), F32)
            for i in range(PC // CH):
                rows = slice(i * CH, (i + 1) * CH)
                lg = logit[b, rows, :]
                target = base[b, rows, :] * rs * two(colb[rows, :])
                lsum = lsum + jnp.sum((target * (lg - log_tot)).reshape(CH // 8, 8, 2 * SH), axis=0)
                gbuf[rows, :] = ((jnp.exp(lg) * inv_tot - target) * factor).astype(BF16)
            lossv[...] += lsum[:, :SH] + lsum[:, SH:]
            gs = dot(wn[0], gbuf[:CB, :]) + dot(wn[1], gbuf[CB:, :])
            part_a[yy, 2 * xp] = gs[:DH, :SH]
            part_a[yy, 2 * xp + 1] = gs[:DH, SH:]
            part_b[2 * xp, yy] = gs[DH:, :SH]
            part_b[2 * xp + 1, yy] = gs[DH:, SH:]

            @pl.when(k < NY - 1)
            def _():
                a_copy(yy, xp, y).start()

            for h in range(2):
                @pl.when(2 * xp + h != x)
                def _():
                    b_copy(2 * xp + h, yy, x).start()

            un = sn[b]
            for i, (cc, h) in enumerate(chunks):
                gw[cc, :, h * CH:(h + 1) * CH] += dot(un, gbuf[i * CH:(i + 1) * CH, :], ((1,), (1,)))

        each(0, HX, pair)

    each(0, NY, grad_rows)

    gw_copy = rcopy(gw.at[oc], gw_in, gw_sem.at[0], gw_sem.at[1], peer)
    gw_copy.start()

    plane_loss[p] = lossv[...]

    def l_copy(q, src):
        slot = plane_loss.at[src]
        return rcopy(slot, slot, l_send.at[q], l_recv.at[src], (q, j))

    each(1, NP, lambda k: l_copy(nxt(p, k, NP), p).start())

    gw_copy.wait_recv()
    for h in range(CB // CH):
        s = slice(h * CH, (h + 1) * CH)
        u, inv = unit_cols(wraw[c, :, s])
        g = gw[c, :, s] + gw_in[:, s]
        gp_all[:, s] = inv * (g - u * jnp.sum(u * g, axis=0, keepdims=True))

    my_cols = pl.ds(pl.multiple_of(p * CB, CB), CB)

    def gp_copy(k):
        q = nxt(p, k, NP)
        rows = pl.ds(pl.multiple_of(q * DB, DB), DB)
        return rcopy(gp_all.at[rows], gp_ref.at[:, my_cols], gp_send.at[q], gp_recv.at[p], (q, j))

    def a_wait(k):
        src = nxt(y, k, NY)
        each(0, HX, lambda xp: a_copy(src, xp, src).wait_recv())

    each(1, NY, a_wait)

    def a_sum(xx):
        t = part_a[y, xx]
        for k in range(1, NY):
            t = t + in_a[nxt(y, k, NY), xx]
        sum_a[xx] = t

    each(0, NX, a_sum)

    def a2_copy(xx, src):
        return rcopy(sum_a.at[xx], in_a2.at[src], a2_send.at[xx], a2_recv.at[src], (dp_of(y, xx), j))

    def a2_start(k):
        a2_copy(nxt(x, k, NX), x).start()

    each(1, NX, a2_start)

    def b_wait(k):
        src = nxt(x, k, NX)
        each(0, NY, lambda yy: b_copy(src, yy, src).wait_recv())

    each(1, NX, b_wait)

    def b_sum(yy):
        t = part_b[x, yy]
        for k in range(1, NX):
            t = t + in_b[nxt(x, k, NX), yy]
        sum_b[yy] = t

    each(0, NY, b_sum)

    def b2_copy(yy, src):
        return rcopy(sum_b.at[yy], in_b2.at[src], b2_send.at[yy], b2_recv.at[src], (dp_of(yy, x), j))

    def b2_start(k):
        b2_copy(nxt(y, k, NY), y).start()

    each(1, NY, b2_start)
    each(1, NP, lambda k: gp_copy(k).start())
    gp_ref[:, my_cols] = gp_all[w_rows, :]

    def l_wait(k):
        q = nxt(p, k, NP)
        l_copy(q, q).wait_recv()

    each(1, NP, l_wait)
    loss_part = plane_loss[0]
    for q in range(1, NP):
        loss_part = loss_part + plane_loss[q]

    def a2_wait(k):
        src = nxt(x, k, NX)
        a2_copy(src, src).wait_recv()

    def b2_wait(k):
        src = nxt(y, k, NY)
        b2_copy(src, src).wait_recv()

    each(1, NX, a2_wait)
    each(1, NY, b2_wait)
    su, sinv = unit_cols(feats[1, y, x])
    ga, gb = sum_a[x], sum_b[y]
    for k in range(1, NX):
        ga = ga + in_a2[nxt(x, k, NX)]
        gb = gb + in_b2[nxt(y, k, NY)]
    dots = jnp.sum(su[:DH] * ga, axis=0, keepdims=True) + jnp.sum(su[DH:] * gb, axis=0, keepdims=True)

    for q in range(NJ):
        lo = q * DB
        msg[q, :DB, :] = ga[lo:lo + DB] if lo < DH else gb[lo - DH:lo - DH + DB]
        msg[q, DB:DB + 8, :] = loss_part
        msg[q, DB + 8:DB + 16, :] = jnp.broadcast_to(dots, (8, SH))
        msg[q, DB + 16:, :] = jnp.broadcast_to(sinv, (8, SH))

    def m_copy(q, src):
        return rcopy(msg.at[q], msg_in.at[src], m_send.at[q], m_recv.at[src], (p, q))

    def m_start(k):
        m_copy(nxt(j, k, NJ), j).start()

    each(1, NJ, m_start)
    msg_in[j] = msg[j]

    def m_wait(k):
        src = nxt(j, k, NJ)
        m_copy(src, src).wait_recv()

    each(1, NJ, m_wait)
    loss_sum = jnp.zeros((8, SH), F32)
    for h in range(2):
        t = msg_in[h, :DB + 16, :]
        for q in range(1, NZ):
            t = t + msg_in[2 * q + h, :DB + 16, :]
        loss_sum = loss_sum + t[DB:DB + 8]
        dsum = t[DB + 8:DB + 9]
        inv = msg_in[h, DB + 16:DB + 17, :]
        own = x_ref[1, :, h * SH:(h + 1) * SH].astype(F32) * inv
        gs_ref[:, h * SH:(h + 1) * SH] = inv * (t[:DB] - own * dsum)
    loss_ref[...] = jnp.full((8, SH), -inv_rows, F32) * jnp.sum(loss_sum)

    def gp_wait(k):
        q = nxt(p, k, NP)
        cols = pl.ds(pl.multiple_of(q * CB, CB), CB)
        rcopy(gp_all.at[pl.ds(0, DB)], gp_ref.at[:, cols], gp_send.at[q], gp_recv.at[q], (q, j)).wait_recv()

    each(1, NP, gp_wait)

    w_core.wait_send()
    gw_copy.wait_send()
    for r in range(ITERS):
        rcopy(core_col.at[r, c], core_col.at[r, c], cc_send.at[r], cc_recv.at[r], peer).wait_send()
        n = 2 * NP if r == 1 else NP
        slot = plane_row.at[r, p, pl.ds(0, n)]
        each(1, NP, lambda k: rcopy(slot, slot, pr_send.at[r, nxt(p, k, NP)], pr_recv.at[r, p], peer).wait_send())
        zslot = z_row.at[r, z, pl.ds(0, n)]
        each(1, NZ, lambda k: rcopy(zslot, zslot, zr_send.at[r, nxt(z, k, NZ)], zr_recv.at[r, z], peer).wait_send())
    each(1, NJ, lambda k: feat_copy(k).wait_send())
    each(1, NP, lambda k: w_copy(k).wait_send())
    each(0, t_send.shape[0], lambda n: t_copy(x, n, peer).wait_send())
    each(0, s_send.shape[0], lambda n: s_copy(y, n, peer).wait_send())
    each(1, NP, lambda k: gp_copy(k).wait_send())
    each(1, NP, lambda k: l_copy(nxt(p, k, NP), p).wait_send())
    each(1, NJ, lambda k: m_copy(nxt(j, k, NJ), j).wait_send())
    each(1, NX, lambda k: a2_copy(nxt(x, k, NX), x).wait_send())
    each(1, NY, lambda k: b2_copy(nxt(y, k, NY), y).wait_send())
    each(1, NY, lambda k: each(0, HX, lambda xp: a_copy(nxt(y, k, NY), xp, y).wait_send()))
    each(1, NX, lambda k: each(0, NY, lambda yy: b_copy(nxt(x, k, NX), yy, x).wait_send()))


def body(cfg, teacher_feats, student_feats, prototypes):
    NP, NJ, NY, NX, _, _ = cfg
    NZ = NJ // 2
    xt = jnp.stack([teacher_feats.T, student_feats.T])
    DB, SB = xt.shape[1:]
    SH = SB // 2
    D = DB * NJ
    DH = D // 2
    WC = prototypes.shape[1]
    CB = WC // NP
    PC = 2 * CB
    NB = NP // 2
    V, S = pltpu.VMEM, pltpu.SemaphoreType.DMA
    scratch = [
        V((2, NY, NX, D, SH), BF16), V((2, D, CB), BF16), V((2, D, CB), BF16), V((2, CB, D), BF16),
        V((NB, D, SB), BF16), V((NB, PC, SB), F32), V((NB, PC, SB), F32), V((PC, SH), F32),
        V((PC, SH), F32), V((NP, SH), F32), V((NP, SH), F32), V((PC, SB), BF16), V((8, SH), F32),
        V((ITERS, 2, 1, PC), F32), V((ITERS, NP, 2 * NP, SH), F32), V((ITERS, NZ, 2 * NP, SH), F32),
        V((2, D, CB), F32), V((D, CB), F32), V((D, CB), F32),
        V((NY, NX, DH, SH), F32), V((NX, NY, DH, SH), F32), V((NY, NX, DH, SH), F32), V((NX, NY, DH, SH), F32),
        V((NX, DH, SH), F32), V((NY, DH, SH), F32), V((NX, DH, SH), F32), V((NY, DH, SH), F32),
        V((NJ, DB + 24, SH), F32), V((NJ, DB + 24, SH), F32), V((NP, 8, SH), F32),
        S((NJ,)), S((NJ,)), S((NP,)), S((NP,)), S((2,)),
        S((NP - 1,)), S((NY, NX)), S((NP - 1,)), S((NY, NX)),
        S((ITERS,)), S((ITERS,)), S((ITERS, NP)), S((ITERS, NP)), S((ITERS, NZ)), S((ITERS, NZ)),
        S((2,)), S((NP,)), S((NP,)),
        S((NB,)), S((NB,)), S((NX, NY)), S((NX, NY)), S((NX,)), S((NX,)), S((NY,)), S((NY,)),
        S((NJ,)), S((NJ,)), S((NP,)), S((NP,)),
    ]
    vmem = pl.BlockSpec(memory_space=pltpu.VMEM)
    loss, gp, gs = pl.pallas_call(
        functools.partial(kernel, cfg),
        out_shape=(
            jax.ShapeDtypeStruct((8, SH), F32),
            jax.ShapeDtypeStruct((DB, WC), F32),
            jax.ShapeDtypeStruct((DB, SB), F32),
        ),
        in_specs=[vmem, vmem],
        out_specs=(vmem, vmem, vmem),
        scratch_shapes=scratch,
        compiler_params=pltpu.CompilerParams(
            collective_id=0, has_side_effects=True, vmem_limit_bytes=56 * 1024 * 1024
        ),
    )(xt, prototypes)
    return loss[0, 0], gp, gs.T


def solution(mesh):
    NP, NJ = mesh.shape["dp"], mesh.shape["proto"]
    NY = NX = int(round(NP ** 0.5))

    def run(teacher_feats, student_feats, prototypes):
        rows, protos = teacher_feats.shape[0], prototypes.shape[1]
        loss_scale = rows * protos // 256
        factor = float(loss_scale) / float(rows) / STUDENT_TEMP
        cfg = (NP, NJ, NY, NX, factor, 1.0 / rows)
        spec = P("dp", "proto")
        return jax.shard_map(
            functools.partial(body, cfg), mesh=mesh, in_specs=(spec,) * 3,
            out_specs=(P(), spec, spec), check_vma=False,
        )(teacher_feats, student_feats, prototypes)

    return run
```

time: 656 us -> 126 us (0.19)
  the two profiles are of different devices: /device:TPU:8 before, /device:TPU:1 now
where the time goes in v1:
time: 126 us; the launch traced here: 125 us
  Pallas kernels  120 us (95%)
  local copies, waits for them, and re-layouts  3.68 us (3%)
  other arithmetic  1.32 us (1%)
    pallas_call x1, Pallas kernels, body(): pl.pallas_call(functools.partial(kernel, cfg), out_shape=(jax.ShapeDtypeS...  120 us

profile of v1, /device:TPU:1, one launch (start us, length us, event | category | flops | bytes accessed | tf_op | source)
XLA Modules:
  0.0 125.2 jit_solution(9794314451825108874)
XLA Ops:
  0.6 1.3 %pad_maximum_fusion.x_ref = bf16[2,16,256]{2,1,0:T(8,128)(2,1)} fusion(bf16[1,16,256]{2,1,0:T(8,128)(2,1)} %bitcast.9, bf16[1,16,256]{2,1,0:T(8,128)(2,1)} %bitcast.10), kind=kLoop, calls=%fused_computation | loop fusion | flops 8192 | bytes 32768 | tf_op jit(solution)/shard_map/stack | solution.py:540
  2.0 119.5 %shard_map.58 = (f32[8,128]{1,0:T(8,128)}, f32[16,8192]{1,0:T(8,128)}, f32[16,256]{1,0:T(8,128)}) custom-call(bf16[2,16,256]{2,1,0:T(8,128)(2,1)} %pad_maximum_fusion.x_ref, bf16[16,8192]{1,0:T(8,128)(2,1)} %w_ref.1), custom_call_target="tpu_custom_call" | custom-call | tf_op jit(solution)/shard_map/pallas_call | solution.py:567
  121.5 1.2 slice.3
  122.7 0.0 copy-start
  122.7 1.9 %copy.8 = f32[16,8192]{1,0:T(8,128)} copy(f32[16,8192]{1,0:T(8,128)} %get-tuple-element.13) | data formatting | bytes 1048576
  124.5 0.0 copy-done
  124.6 0.6 copy.9
Async XLA Ops:
  122.7 1.9 %copy-start = (f32[16,256]{1,0:T(8,128)S(1)}, f32[16,256]{1,0:T(8,128)}, u32[]{:S(2)}) copy-start(f32[16,256]{1,0:T(8,128)} %get-tuple-element.8) | copy-start | bytes 49156

commit v2 on v1

--- a/solution.py
+++ b/solution.py
@@ -35,19 +35,19 @@
 
 
 def kernel(
-    cfg, x_ref, w_ref, loss_ref, gp_ref, gs_ref,
+    cfg, t_ref, s_ref, w_ref, loss_ref, gp_ref, gs_ref,
     feats, wraw, wn, wtn, sn, base, logit, acc, colb, rscale, tots, gbuf, lossv,
     core_col, plane_row, z_row, gw, gw_in, gp_all,
     part_a, part_b, in_a, in_b, sum_a, sum_b, in_a2, in_b2, msg, msg_in, plane_loss,
-    f_send, f_recv, w_send, w_recv, wc_sem, t_send, t_recv, s_send, s_recv,
+    f_send, f_recv, w_send, w_recv, wc_sem, ag_send, ag_recv, own_sem,
     cc_send, cc_recv, pr_send, pr_recv, zr_send, zr_recv, gw_sem, gp_send, gp_recv,
     a_send, a_recv, b_send, b_recv, a2_send, a2_recv, b2_send, b2_recv,
     m_send, m_recv, l_send, l_recv,
 ):
     NP, NJ, NY, NX, factor, inv_rows = cfg
     NZ = NJ // 2
-    DB = x_ref.shape[1]
-    SH = x_ref.shape[2] // 2
+    DB = t_ref.shape[0]
+    SH = t_ref.shape[1] // 2
     CB = wraw.shape[2]
     D = DB * NJ
     DH = D // 2
@@ -79,16 +79,16 @@
     each(1, NJ, greet_proto)
     pl.semaphore_wait(barrier, NP + NJ - 2)
 
-    def half(cc):
-        return x_ref.at[:, :, pl.ds(pl.multiple_of(cc * SH, SH), SH)]
-
     my_rows = pl.ds(pl.multiple_of(j * DB, DB), DB)
-
-    def feat_copy(k):
+    my_half = pl.ds(pl.multiple_of(c * SH, SH), SH)
+
+    def feat_copy(arr, k):
         q = nxt(j, k, NJ)
-        return rcopy(half(lax.rem(q, 2)), feats.at[:, y, x, my_rows], f_send.at[q], f_recv.at[j], (p, q))
-
-    each(1, NJ, lambda k: feat_copy(k).start())
+        lanes = pl.ds(pl.multiple_of(lax.rem(q, 2) * SH, SH), SH)
+        src = (t_ref, s_ref)[arr].at[:, lanes]
+        return rcopy(src, feats.at[arr, y, x, my_rows], f_send.at[arr, q], f_recv.at[arr, j], (p, q))
+
+    each(1, NJ, lambda k: feat_copy(0, k).start())
 
     w_rows = pl.ds(pl.multiple_of(p * DB, DB), DB)
 
@@ -98,40 +98,69 @@
         return rcopy(w_ref.at[:, cols], wraw.at[c, w_rows], w_send.at[q], w_recv.at[p], (q, j))
 
     each(1, NP, lambda k: w_copy(k).start())
-    feats[:, y, x, my_rows, :] = x_ref[:, :, pl.ds(pl.multiple_of(c * SH, SH), SH)]
-    wraw[c, w_rows, :] = w_ref[:, pl.ds(pl.multiple_of(p * CB, CB), CB)]
-
-    def feat_wait(k):
-        q = nxt(j, k, NJ)
-        rows = pl.ds(pl.multiple_of(q * DB, DB), DB)
-        rcopy(half(0), feats.at[:, y, x, rows], f_send.at[q], f_recv.at[q], (p, q)).wait_recv()
-
-    each(1, NJ, feat_wait)
-
-    def t_copy(xs, n, dev):
-        slot = feats.at[0, y, xs]
-        return rcopy(slot, slot, t_send.at[n], t_recv.at[y, xs], dev)
-
-    def s_copy(ys, n, dev):
-        slot = feats.at[1, ys, x]
-        return rcopy(slot, slot, s_send.at[n], s_recv.at[ys, x], dev)
-
-    def t_wait(yy, xx):
-        slot = feats.at[0, yy, xx]
-        rcopy(slot, slot, t_send.at[0], t_recv.at[yy, xx], peer).wait_recv()
-
-    def s_wait(yy, xx):
-        slot = feats.at[1, yy, xx]
-        rcopy(slot, slot, s_send.at[0], s_recv.at[yy, xx], peer).wait_recv()
-
-    def own_out(k):
-        xq, yq = nxt(x, k, NX), nxt(y, k, NY)
-        t_copy(x, k - 1, (dp_of(y, xq), j)).start()
-        s_copy(y, k - 1, (dp_of(yq, x), j)).start()
-        t_copy(x, NX - 2 + k, (dp_of(yq, x), j)).start()
-        s_copy(y, NY - 2 + k, (dp_of(y, xq), j)).start()
-
-    each(1, NX, own_out)
+    each(1, NJ, lambda k: feat_copy(1, k).start())
+    feats[0, y, x, my_rows, :] = t_ref[:, my_half]
+    feats[1, y, x, my_rows, :] = s_ref[:, my_half]
+    w_own = pltpu.make_async_copy(
+        w_ref.at[:, pl.ds(pl.multiple_of(p * CB, CB), CB)], wraw.at[c, w_rows], own_sem.at[0])
+    w_own.start()
+
+    def feat_wait(arr):
+        def wait(k):
+            q = nxt(j, k, NJ)
+            rows = pl.ds(pl.multiple_of(q * DB, DB), DB)
+            rcopy(t_ref.at[:, pl.ds(0, SH)], feats.at[arr, y, x, rows],
+                  f_send.at[arr, q], f_recv.at[arr, q], (p, q)).wait_recv()
+        each(1, NJ, wait)
+
+    near = sorted(range(1, NX), key=lambda k: min(k, NX - k))
+
+    def ag_copy(arr, h, ys, xs, n, dev):
+        slot = feats.at[arr, ys, xs, pl.ds(h * DH, DH)]
+        return rcopy(slot, slot, ag_send.at[2 * arr + h, n], ag_recv.at[2 * arr + h, ys, xs], dev)
+
+    def ag_wait(arr, h, ys, xs):
+        ag_copy(arr, h, ys, xs, 0, peer).wait_recv()
+
+    def own_out(arr):
+        for i, k in enumerate(near):
+            ag_copy(arr, 0, y, x, i, (dp_of(y, nxt(x, k, NX)), j)).start()
+            ag_copy(arr, 1, y, x, i, (dp_of(nxt(y, k, NY), x), j)).start()
+        for i, k in enumerate(near):
+            ag_copy(arr, 0, y, x, NX - 1 + i, (dp_of(nxt(y, k, NY), x), j)).start()
+            ag_copy(arr, 1, y, x, NX - 1 + i, (dp_of(y, nxt(x, k, NX)), j)).start()
+
+    def forward(arr):
+        for i, k in enumerate(near):
+            xs, ys = nxt(x, k, NX), nxt(y, k, NY)
+            n0 = (2 + i) * (NX - 1) - 1
+            ag_wait(arr, 0, y, xs)
+            each(1, NY, lambda m: ag_copy(arr, 0, y, xs, n0 + m, (dp_of(nxt(y, m, NY), x), j)).start())
+            ag_wait(arr, 1, ys, x)
+            each(1, NX, lambda m: ag_copy(arr, 1, ys, x, n0 + m, (dp_of(y, nxt(x, m, NX)), j)).start())
+
+    def pair_wait(arr, yy, xp):
+        def one(xx):
+            @pl.when(yy != y)
+            def _():
+                @pl.when(xx != x)
+                def _():
+                    ag_wait(arr, 0, yy, xx)
+                    ag_wait(arr, 1, yy, xx)
+
+                @pl.when(xx == x)
+                def _():
+                    ag_wait(arr, 0, yy, xx)
+
+            @pl.when(jnp.logical_and(yy == y, xx != x))
+            def _():
+                ag_wait(arr, 1, yy, xx)
+
+        one(2 * xp)
+        one(2 * xp + 1)
+
+    feat_wait(0)
+    own_out(0)
 
     def w_wait(k):
         q = nxt(p, k, NP)
@@ -139,26 +168,12 @@
         rcopy(w_ref.at[:, pl.ds(0, CB)], wraw.at[c, rows], w_send.at[q], w_recv.at[q], (q, j)).wait_recv()
 
     each(1, NP, w_wait)
+    w_own.wait()
     w_core = rcopy(wraw.at[c], wraw.at[c], wc_sem.at[0], wc_sem.at[1], peer)
     w_core.start()
-
-    def forward(k):
-        xs, ys = nxt(x, k, NX), nxt(y, k, NY)
-        t_wait(y, xs)
-        n0 = 2 * (NX - 1) + (k - 1) * (NX - 1) - 1
-
-        def fwd_t(m):
-            t_copy(xs, n0 + m, (dp_of(nxt(y, m, NY), x), j)).start()
-
-        each(1, NY, fwd_t)
-        s_wait(ys, x)
-
-        def fwd_s(m):
-            s_copy(ys, n0 + m, (dp_of(y, nxt(x, m, NX)), j)).start()
-
-        each(1, NX, fwd_s)
-
-    each(1, NX, forward)
+    forward(0)
+    feat_wait(1)
+    own_out(1)
 
     def unit_cols(v):
         v32 = v.astype(F32)
@@ -183,13 +198,10 @@
     acc[...] = jnp.zeros_like(acc)
 
     def teacher_rows(k):
-        yy = nxt(y, k, NY)
-
-        @pl.when(k > 0)
-        def _():
-            each(0, NX, lambda xx: t_wait(yy, xx))
+        yy = nxt(y, k + k // 2 - 2 * (k // 3), NY)
 
         def pair(xp):
+            pair_wait(0, yy, xp)
             b = yy * HX + xp
             raw = jnp.concatenate([feats[0, yy, 2 * xp], feats[0, yy, 2 * xp + 1]], axis=1)
             u, _ = unit_cols(raw)
@@ -210,13 +222,7 @@
         def pair(xp):
             b = yy * HX + xp
 
-            def arrive(xx):
-                @pl.when(jnp.logical_and(k >= 0, xx != x))
-                def _():
-                    s_wait(yy, xx)
-
-            arrive(2 * xp)
-            arrive(2 * xp + 1)
+            pair_wait(1, yy, xp)
             raw = jnp.concatenate([feats[1, yy, 2 * xp], feats[1, yy, 2 * xp + 1]], axis=1)
             u, _ = unit_cols(raw)
             un = u.astype(BF16)
@@ -272,8 +278,8 @@
         each(0, NP // 2, pair)
 
     def row_exchange(r, between=None):
-        n = 2 * NP if r == 1 else NP
-        if r == 1:
+        n = 2 * NP if r == 2 else NP
+        if r == 2:
             plane_row[r, p, NP:, :] = tots[...]
 
         def plane_copy(q, src):
@@ -309,7 +315,7 @@
         for q in range(1, NZ):
             total = total + z_row[r, q, :n, :]
         rscale[...] = 1.0 / total[:NP]
-        if r == 1:
+        if r == 2:
             tots[...] = total[NP:]
 
     for r in range(ITERS):
@@ -317,7 +323,7 @@
             col_pass()
         col_exchange(r)
         row_pass(r)
-        row_exchange(r, (lambda: each(0, NY, student_rows)) if r == 0 else None)
+        row_exchange(r, (lambda: forward(1), lambda: each(0, NY, student_rows), None)[r])
 
     lossv[...] = jnp.zeros_like(lossv)
     gw[...] = jnp.zeros_like(gw)
@@ -400,51 +406,47 @@
         rows = pl.ds(pl.multiple_of(q * DB, DB), DB)
         return rcopy(gp_all.at[rows], gp_ref.at[:, my_cols], gp_send.at[q], gp_recv.at[p], (q, j))
 
-    def a_wait(k):
-        src = nxt(y, k, NY)
-        each(0, HX, lambda xp: a_copy(src, xp, src).wait_recv())
-
-    each(1, NY, a_wait)
-
-    def a_sum(xx):
-        t = part_a[y, xx]
+    def a_sum(xp):
         for k in range(1, NY):
-            t = t + in_a[nxt(y, k, NY), xx]
-        sum_a[xx] = t
-
-    each(0, NX, a_sum)
+            src = nxt(y, k, NY)
+            a_copy(src, xp, src).wait_recv()
+        for h in range(2):
+            xx = 2 * xp + h
+            t = part_a[y, xx]
+            for k in range(1, NY):
+                t = t + in_a[nxt(y, k, NY), xx]
+            sum_a[xx] = t
+
+            @pl.when(xx != x)
+            def _():
+                a2_copy(xx, x).start()
 
     def a2_copy(xx, src):
         return rcopy(sum_a.at[xx], in_a2.at[src], a2_send.at[xx], a2_recv.at[src], (dp_of(y, xx), j))
 
-    def a2_start(k):
-        a2_copy(nxt(x, k, NX), x).start()
-
-    each(1, NX, a2_start)
-
-    def b_wait(k):
-        src = nxt(x, k, NX)
-        each(0, NY, lambda yy: b_copy(src, yy, src).wait_recv())
-
-    each(1, NX, b_wait)
-
     def b_sum(yy):
+        for k in range(1, NX):
+            src = nxt(x, k, NX)
+            b_copy(src, yy, src).wait_recv()
         t = part_b[x, yy]
         for k in range(1, NX):
             t = t + in_b[nxt(x, k, NX), yy]
         sum_b[yy] = t
 
-    each(0, NY, b_sum)
-
     def b2_copy(yy, src):
         return rcopy(sum_b.at[yy], in_b2.at[src], b2_send.at[yy], b2_recv.at[src], (dp_of(yy, x), j))
 
-    def b2_start(k):
-        b2_copy(nxt(y, k, NY), y).start()
-
-    each(1, NY, b2_start)
+    def b_next(k):
+        yy = nxt(y, k, NY)
+        b_sum(yy)
+        b2_copy(yy, y).start()
+
+    each(1, NY, b_next)
+    each(0, HX, a_sum)
+    b_sum(y)
     each(1, NP, lambda k: gp_copy(k).start())
-    gp_ref[:, my_cols] = gp_all[w_rows, :]
+    gp_own = pltpu.make_async_copy(gp_all.at[w_rows], gp_ref.at[:, my_cols], own_sem.at[1])
+    gp_own.start()
 
     def l_wait(k):
         q = nxt(p, k, NP)
@@ -454,6 +456,8 @@
     loss_part = plane_loss[0]
     for q in range(1, NP):
         loss_part = loss_part + plane_loss[q]
+
+    loss_row = jnp.sum(loss_part, axis=0, keepdims=True)
 
     def a2_wait(k):
         src = nxt(x, k, NX)
@@ -475,9 +479,10 @@
     for q in range(NJ):
         lo = q * DB
         msg[q, :DB, :] = ga[lo:lo + DB] if lo < DH else gb[lo - DH:lo - DH + DB]
-        msg[q, DB:DB + 8, :] = loss_part
-        msg[q, DB + 8:DB + 16, :] = jnp.broadcast_to(dots, (8, SH))
-        msg[q, DB + 16:, :] = jnp.broadcast_to(sinv, (8, SH))
+        msg[q, DB:DB + 1, :] = dots
+        msg[q, DB + 1:DB + 2, :] = sinv
+        msg[q, DB + 2:DB + 3, :] = loss_row
+        msg[q, DB + 3:, :] = jnp.zeros((5, SH), F32)
 
     def m_copy(q, src):
         return rcopy(msg.at[q], msg_in.at[src], m_send.at[q], m_recv.at[src], (p, q))
@@ -493,17 +498,17 @@
         m_copy(src, src).wait_recv()
 
     each(1, NJ, m_wait)
-    loss_sum = jnp.zeros((8, SH), F32)
+    loss_sum = jnp.zeros((1, SH), F32)
     for h in range(2):
-        t = msg_in[h, :DB + 16, :]
+        t = msg_in[h]
         for q in range(1, NZ):
-            t = t + msg_in[2 * q + h, :DB + 16, :]
-        loss_sum = loss_sum + t[DB:DB + 8]
-        dsum = t[DB + 8:DB + 9]
-        inv = msg_in[h, DB + 16:DB + 17, :]
-        own = x_ref[1, :, h * SH:(h + 1) * SH].astype(F32) * inv
+            t = t + msg_in[2 * q + h]
+        loss_sum = loss_sum + t[DB + 2:DB + 3]
+        dsum = t[DB:DB + 1]
+        inv = msg_in[h, DB + 1:DB + 2, :]
+        own = s_ref[:, h * SH:(h + 1) * SH].astype(F32) * inv
         gs_ref[:, h * SH:(h + 1) * SH] = inv * (t[:DB] - own * dsum)
-    loss_ref[...] = jnp.full((8, SH), -inv_rows, F32) * jnp.sum(loss_sum)
+    loss_ref[0, 0] = -inv_rows * jnp.sum(loss_sum)
 
     def gp_wait(k):
         q = nxt(p, k, NP)
@@ -511,20 +516,22 @@
         rcopy(gp_all.at[pl.ds(0, DB)], gp_ref.at[:, cols], gp_send.at[q], gp_recv.at[q], (q, j)).wait_recv()
 
     each(1, NP, gp_wait)
+    gp_own.wait()
 
     w_core.wait_send()
     gw_copy.wait_send()
     for r in range(ITERS):
         rcopy(core_col.at[r, c], core_col.at[r, c], cc_send.at[r], cc_recv.at[r], peer).wait_send()
-        n = 2 * NP if r == 1 else NP
+        n = 2 * NP if r == 2 else NP
         slot = plane_row.at[r, p, pl.ds(0, n)]
         each(1, NP, lambda k: rcopy(slot, slot, pr_send.at[r, nxt(p, k, NP)], pr_recv.at[r, p], peer).wait_send())
         zslot = z_row.at[r, z, pl.ds(0, n)]
         each(1, NZ, lambda k: rcopy(zslot, zslot, zr_send.at[r, nxt(z, k, NZ)], zr_recv.at[r, z], peer).wait_send())
-    each(1, NJ, lambda k: feat_copy(k).wait_send())
+    for arr in range(2):
+        each(1, NJ, lambda k: feat_copy(arr, k).wait_send())
+        for h in range(2):
+            each(0, NP - 1, lambda n: ag_copy(arr, h, y, x, n, peer).wait_send())
     each(1, NP, lambda k: w_copy(k).wait_send())
-    each(0, t_send.shape[0], lambda n: t_copy(x, n, peer).wait_send())
-    each(0, s_send.shape[0], lambda n: s_copy(y, n, peer).wait_send())
     each(1, NP, lambda k: gp_copy(k).wait_send())
     each(1, NP, lambda k: l_copy(nxt(p, k, NP), p).wait_send())
     each(1, NJ, lambda k: m_copy(nxt(j, k, NJ), j).wait_send())
@@ -537,8 +544,7 @@
 def body(cfg, teacher_feats, student_feats, prototypes):
     NP, NJ, NY, NX, _, _ = cfg
     NZ = NJ // 2
-    xt = jnp.stack([teacher_feats.T, student_feats.T])
-    DB, SB = xt.shape[1:]
+    SB, DB = teacher_feats.shape
     SH = SB // 2
     D = DB * NJ
     DH = D // 2
@@ -555,29 +561,30 @@
         V((2, D, CB), F32), V((D, CB), F32), V((D, CB), F32),
         V((NY, NX, DH, SH), F32), V((NX, NY, DH, SH), F32), V((NY, NX, DH, SH), F32), V((NX, NY, DH, SH), F32),
         V((NX, DH, SH), F32), V((NY, DH, SH), F32), V((NX, DH, SH), F32), V((NY, DH, SH), F32),
-        V((NJ, DB + 24, SH), F32), V((NJ, DB + 24, SH), F32), V((NP, 8, SH), F32),
-        S((NJ,)), S((NJ,)), S((NP,)), S((NP,)), S((2,)),
-        S((NP - 1,)), S((NY, NX)), S((NP - 1,)), S((NY, NX)),
+        V((NJ, DB + 8, SH), F32), V((NJ, DB + 8, SH), F32), V((NP, 8, SH), F32),
+        S((2, NJ)), S((2, NJ)), S((NP,)), S((NP,)), S((2,)),
+        S((4, NP - 1)), S((4, NY, NX)), S((2,)),
         S((ITERS,)), S((ITERS,)), S((ITERS, NP)), S((ITERS, NP)), S((ITERS, NZ)), S((ITERS, NZ)),
         S((2,)), S((NP,)), S((NP,)),
         S((NB,)), S((NB,)), S((NX, NY)), S((NX, NY)), S((NX,)), S((NX,)), S((NY,)), S((NY,)),
         S((NJ,)), S((NJ,)), S((NP,)), S((NP,)),
     ]
     vmem = pl.BlockSpec(memory_space=pltpu.VMEM)
+    hbm = pl.BlockSpec(memory_space=pl.ANY)
     loss, gp, gs = pl.pallas_call(
         functools.partial(kernel, cfg),
         out_shape=(
-            jax.ShapeDtypeStruct((8, SH), F32),
+            jax.ShapeDtypeStruct((1, 1), F32),
             jax.ShapeDtypeStruct((DB, WC), F32),
             jax.ShapeDtypeStruct((DB, SB), F32),
         ),
-        in_specs=[vmem, vmem],
-        out_specs=(vmem, vmem, vmem),
+        in_specs=[vmem, vmem, hbm],
+        out_specs=(pl.BlockSpec(memory_space=pltpu.SMEM), hbm, vmem),
         scratch_shapes=scratch,
         compiler_params=pltpu.CompilerParams(
             collective_id=0, has_side_effects=True, vmem_limit_bytes=56 * 1024 * 1024
         ),
-    )(xt, prototypes)
+    )(teacher_feats.T, student_feats.T, prototypes)
     return loss[0, 0], gp, gs.T
 
 

time: 126 us -> 112 us (0.89)
  the two profiles are of different devices: /device:TPU:1 before, /device:TPU:8 now
where the time goes in v2:
time: 112 us; the launch traced here: 111 us
  Pallas kernels  106 us (95%)
  local copies, waits for them, and re-layouts  2.48 us (2%)
  between operations  2.38 us (2%)
    pallas_call x1, Pallas kernels, body(): pl.pallas_call(functools.partial(kernel, cfg), out_shape=(jax.ShapeDtypeS...  106 us
    unnamed x4, local copies, waits for them, and re-layouts  2.48 us

profile of v2, /device:TPU:8, one launch (start us, length us, event | category | flops | bytes accessed | tf_op | source)
XLA Modules:
  0.0 110.7 jit_solution(16208028152110450544)
XLA Ops:
  0.6 105.8 %shard_map.58 = (f32[1,1]{1,0:T(1,128)}, f32[16,8192]{1,0:T(8,128)}, f32[16,256]{1,0:T(8,128)}) custom-call(bf16[16,256]{1,0:T(8,128)(2,1)} %bitcast.5, bf16[16,256]{1,0:T(8,128)(2,1)} %bitcast.6, bf16[16,8192]{1,0:T(8,128)(2,1)} %w_ref.1), custom_call_target="tpu_custom_call" | custom-call | tf_op jit(solution)/shard_map/pallas_call | solution.py:574
  107.1 0.0 copy-start
  107.1 1.9 %copy.10 = f32[16,8192]{1,0:T(8,128)} copy(f32[16,8192]{1,0:T(8,128)} %get-tuple-element.13) | data formatting | bytes 1048576
  109.0 0.0 copy-done
  109.0 0.6 copy.11
Async XLA Ops:
  107.1 1.9 %copy-start = (f32[16,256]{1,0:T(8,128)S(1)}, f32[16,256]{1,0:T(8,128)}, u32[]{:S(2)}) copy-start(f32[16,256]{1,0:T(8,128)} %get-tuple-element.8) | copy-start | bytes 49156

commit v3 on v2

--- a/solution.py
+++ b/solution.py
@@ -23,6 +23,10 @@
     )
 
 
+def take(ref, sem):
+    pltpu.make_async_copy(ref, ref, sem).wait()
+
+
 def each(lo, hi, fn):
     def step(k, carry):
         fn(k)
@@ -39,7 +43,7 @@
     feats, wraw, wn, wtn, sn, base, logit, acc, colb, rscale, tots, gbuf, lossv,
     core_col, plane_row, z_row, gw, gw_in, gp_all,
     part_a, part_b, in_a, in_b, sum_a, sum_b, in_a2, in_b2, msg, msg_in, plane_loss,
-    f_send, f_recv, w_send, w_recv, wc_sem, ag_send, ag_recv, own_sem,
+    f_send, f_recv, w_send, w_recv, wc_sem, ag_send, ag_recv, ag_recv_s, own_sem,
     cc_send, cc_recv, pr_send, pr_recv, zr_send, zr_recv, gw_sem, gp_send, gp_recv,
     a_send, a_recv, b_send, b_recv, a2_send, a2_recv, b2_send, b2_recv,
     m_send, m_recv, l_send, l_recv,
@@ -54,6 +58,7 @@
     PC = 2 * CB
     CH = min(256, CB)
     HX = NX // 2
+    ag_rows = (NP - 1) * DH * SH // 2 // (2 * SH)
     p = lax.axis_index("dp")
     j = lax.axis_index("proto")
     y, x = p // NX, lax.rem(p, NX)
@@ -86,7 +91,7 @@
         q = nxt(j, k, NJ)
         lanes = pl.ds(pl.multiple_of(lax.rem(q, 2) * SH, SH), SH)
         src = (t_ref, s_ref)[arr].at[:, lanes]
-        return rcopy(src, feats.at[arr, y, x, my_rows], f_send.at[arr, q], f_recv.at[arr, j], (p, q))
+        return rcopy(src, feats.at[arr, y, x, my_rows], f_send.at[arr], f_recv.at[arr], (p, q))
 
     each(1, NJ, lambda k: feat_copy(0, k).start())
 
@@ -95,7 +100,7 @@
     def w_copy(k):
         q = nxt(p, k, NP)
         cols = pl.ds(pl.multiple_of(q * CB, CB), CB)
-        return rcopy(w_ref.at[:, cols], wraw.at[c, w_rows], w_send.at[q], w_recv.at[p], (q, j))
+        return rcopy(w_ref.at[:, cols], wraw.at[c, w_rows], w_send.at[0], w_recv.at[0], (q, j))
 
     each(1, NP, lambda k: w_copy(k).start())
     each(1, NJ, lambda k: feat_copy(1, k).start())
@@ -106,38 +111,38 @@
     w_own.start()
 
     def feat_wait(arr):
-        def wait(k):
-            q = nxt(j, k, NJ)
-            rows = pl.ds(pl.multiple_of(q * DB, DB), DB)
-            rcopy(t_ref.at[:, pl.ds(0, SH)], feats.at[arr, y, x, rows],
-                  f_send.at[arr, q], f_recv.at[arr, q], (p, q)).wait_recv()
-        each(1, NJ, wait)
+        take(feats.at[arr, y, x, pl.ds(0, D - DB)], f_recv.at[arr])
 
     near = sorted(range(1, NX), key=lambda k: min(k, NX - k))
 
-    def ag_copy(arr, h, ys, xs, n, dev):
+    def ag_copy(arr, h, ys, xs, stage, dev):
         slot = feats.at[arr, ys, xs, pl.ds(h * DH, DH)]
-        return rcopy(slot, slot, ag_send.at[2 * arr + h, n], ag_recv.at[2 * arr + h, ys, xs], dev)
+        sem = ag_recv.at[h, ys, xs] if arr == 0 else ag_recv_s.at[h, stage]
+        return rcopy(slot, slot, ag_send.at[arr, h], sem, dev)
 
     def ag_wait(arr, h, ys, xs):
-        ag_copy(arr, h, ys, xs, 0, peer).wait_recv()
+        take(feats.at[arr, ys, xs, pl.ds(h * DH, DH)], ag_recv.at[h, ys, xs])
 
     def own_out(arr):
-        for i, k in enumerate(near):
-            ag_copy(arr, 0, y, x, i, (dp_of(y, nxt(x, k, NX)), j)).start()
-            ag_copy(arr, 1, y, x, i, (dp_of(nxt(y, k, NY), x), j)).start()
-        for i, k in enumerate(near):
-            ag_copy(arr, 0, y, x, NX - 1 + i, (dp_of(nxt(y, k, NY), x), j)).start()
-            ag_copy(arr, 1, y, x, NX - 1 + i, (dp_of(y, nxt(x, k, NX)), j)).start()
+        for k in near:
+            ag_copy(arr, 0, y, x, 0, (dp_of(y, nxt(x, k, NX)), j)).start()
+            ag_copy(arr, 1, y, x, 0, (dp_of(nxt(y, k, NY), x), j)).start()
+        for k in near:
+            ag_copy(arr, 0, y, x, 1, (dp_of(nxt(y, k, NY), x), j)).start()
+            ag_copy(arr, 1, y, x, 1, (dp_of(y, nxt(x, k, NX)), j)).start()
 
     def forward(arr):
-        for i, k in enumerate(near):
+        if arr == 1:
+            for h in range(2):
+                take(feats.at[1, 0, pl.ds(0, NX - 1), pl.ds(0, DH)], ag_recv_s.at[h, 0])
+        for k in near:
             xs, ys = nxt(x, k, NX), nxt(y, k, NY)
-            n0 = (2 + i) * (NX - 1) - 1
-            ag_wait(arr, 0, y, xs)
-            each(1, NY, lambda m: ag_copy(arr, 0, y, xs, n0 + m, (dp_of(nxt(y, m, NY), x), j)).start())
-            ag_wait(arr, 1, ys, x)
-            each(1, NX, lambda m: ag_copy(arr, 1, ys, x, n0 + m, (dp_of(y, nxt(x, m, NX)), j)).start())
+            if arr == 0:
+                ag_wait(0, 0, y, xs)
+            each(1, NY, lambda m: ag_copy(arr, 0, y, xs, 1, (dp_of(nxt(y, m, NY), x), j)).start())
+            if arr == 0:
+                ag_wait(0, 1, ys, x)
+            each(1, NX, lambda m: ag_copy(arr, 1, ys, x, 1, (dp_of(y, nxt(x, m, NX)), j)).start())
 
     def pair_wait(arr, yy, xp):
         def one(xx):
@@ -162,12 +167,7 @@
     feat_wait(0)
     own_out(0)
 
-    def w_wait(k):
-        q = nxt(p, k, NP)
-        rows = pl.ds(pl.multiple_of(q * DB, DB), DB)
-        rcopy(w_ref.at[:, pl.ds(0, CB)], wraw.at[c, rows], w_send.at[q], w_recv.at[q], (q, j)).wait_recv()
-
-    each(1, NP, w_wait)
+    take(wraw.at[c, pl.ds(0, D - DB)], w_recv.at[0])
     w_own.wait()
     w_core = rcopy(wraw.at[c], wraw.at[c], wc_sem.at[0], wc_sem.at[1], peer)
     w_core.start()
@@ -216,13 +216,11 @@
 
     each(0, NY, teacher_rows)
 
-    def student_rows(k):
-        yy = nxt(y, k, NY)
+    def student_rows(yy):
 
         def pair(xp):
             b = yy * HX + xp
 
-            pair_wait(1, yy, xp)
             raw = jnp.concatenate([feats[1, yy, 2 * xp], feats[1, yy, 2 * xp + 1]], axis=1)
             u, _ = unit_cols(raw)
             un = u.astype(BF16)
@@ -235,8 +233,8 @@
                 part = part + jnp.sum(jnp.exp(v).reshape(CH // 8, 8, 2 * SH), axis=0)
             tot = jnp.sum(part, axis=0, keepdims=True)
             q = yy * NX + 2 * xp
-            tots[pl.ds(q, 1), :] = tot[:, :SH]
-            tots[pl.ds(q + 1, 1), :] = tot[:, SH:]
+            plane_row[ITERS, p, pl.ds(q, 1), :] = tot[:, :SH]
+            plane_row[ITERS, p, pl.ds(q + 1, 1), :] = tot[:, SH:]
 
         each(0, HX, pair)
 
@@ -277,53 +275,48 @@
 
         each(0, NP // 2, pair)
 
-    def row_exchange(r, between=None):
-        n = 2 * NP if r == 2 else NP
+    def plane_start(r):
+        slot = plane_row.at[r, p]
+        each(1, NP, lambda k: rcopy(slot, slot, pr_send.at[r], pr_recv.at[r], (nxt(p, k, NP), j)).start())
+
+    def plane_end(r):
+        take(plane_row.at[r, pl.ds(0, NP - 1)], pr_recv.at[r])
+        total = plane_row[r, 0]
+        for q in range(1, NP):
+            total = total + plane_row[r, q]
+        z_row[r, z] = total
+
+    def z_start(r):
+        slot = z_row.at[r, z]
+        each(1, NZ, lambda k: rcopy(slot, slot, zr_send.at[r], zr_recv.at[r], (p, 2 * nxt(z, k, NZ) + c)).start())
+
+    def z_end(r):
+        take(z_row.at[r, pl.ds(0, NZ - 1)], zr_recv.at[r])
+        total = z_row[r, 0]
+        for q in range(1, NZ):
+            total = total + z_row[r, q]
+        return total
+
+    for r in range(ITERS):
         if r == 2:
-            plane_row[r, p, NP:, :] = tots[...]
-
-        def plane_copy(q, src):
-            slot = plane_row.at[r, src, pl.ds(0, n)]
-            return rcopy(slot, slot, pr_send.at[r, q], pr_recv.at[r, src], (q, j))
-
-        each(1, NP, lambda k: plane_copy(nxt(p, k, NP), p).start())
-        if between is not None:
-            between()
-
-        def plane_wait(k):
-            q = nxt(p, k, NP)
-            plane_copy(q, q).wait_recv()
-
-        each(1, NP, plane_wait)
-        total = plane_row[r, 0, :n, :]
-        for q in range(1, NP):
-            total = total + plane_row[r, q, :n, :]
-        z_row[r, z, :n, :] = total
-
-        def z_copy(q, src):
-            slot = z_row.at[r, src, pl.ds(0, n)]
-            return rcopy(slot, slot, zr_send.at[r, q], zr_recv.at[r, src], (p, 2 * q + c))
-
-        each(1, NZ, lambda k: z_copy(nxt(z, k, NZ), z).start())
-
-        def z_wait(k):
-            q = nxt(z, k, NZ)
-            z_copy(q, q).wait_recv()
-
-        each(1, NZ, z_wait)
-        total = z_row[r, 0, :n, :]
-        for q in range(1, NZ):
-            total = total + z_row[r, q, :n, :]
-        rscale[...] = 1.0 / total[:NP]
-        if r == 2:
-            tots[...] = total[NP:]
-
-    for r in range(ITERS):
+            plane_end(ITERS)
+            z_start(ITERS)
         if r > 0:
             col_pass()
         col_exchange(r)
         row_pass(r)
-        row_exchange(r, (lambda: forward(1), lambda: each(0, NY, student_rows), None)[r])
+        plane_start(r)
+        if r == 0:
+            forward(1)
+        if r == 1:
+            for h in range(2):
+                take(feats.at[1, pl.ds(0, NY - 1), :, pl.ds(0, DH)], ag_recv_s.at[h, 1])
+            each(0, NY, student_rows)
+            plane_start(ITERS)
+        plane_end(r)
+        z_start(r)
+        rscale[...] = 1.0 / z_end(r)
+    tots[...] = z_end(ITERS)
 
     lossv[...] = jnp.zeros_like(lossv)
     gw[...] = jnp.zeros_like(gw)
@@ -331,14 +324,12 @@
     def row_of(ref, q):
         return jnp.concatenate([ref[pl.ds(q, 1), :], ref[pl.ds(q + 1, 1), :]], axis=1)
 
-    def a_copy(yy, xp, src_y):
+    def a_copy(yy, xp):
         xs = pl.ds(2 * xp, 2)
-        n = yy * HX + xp
-        m = src_y * HX + xp
-        return rcopy(part_a.at[yy, xs], in_a.at[src_y, xs], a_send.at[n], a_recv.at[m], (dp_of(yy, x), j))
-
-    def b_copy(xx, yy, src_x):
-        return rcopy(part_b.at[xx, yy], in_b.at[src_x, yy], b_send.at[xx, yy], b_recv.at[src_x, yy], (dp_of(y, xx), j))
+        return rcopy(part_a.at[yy, xs], in_a.at[y, xs], a_send.at[0], a_recv.at[xp], (dp_of(yy, x), j))
+
+    def b_copy(xx, yy):
+        return rcopy(part_b.at[xx, yy], in_b.at[x, yy], b_send.at[0], b_recv.at[yy], (dp_of(y, xx), j))
 
     def grad_rows(k):
         yy = nxt(y, k + 1, NY)
@@ -366,12 +357,12 @@
 
             @pl.when(k < NY - 1)
             def _():
-                a_copy(yy, xp, y).start()
+                a_copy(yy, xp).start()
 
             for h in range(2):
                 @pl.when(2 * xp + h != x)
                 def _():
-                    b_copy(2 * xp + h, yy, x).start()
+                    b_copy(2 * xp + h, yy).start()
 
             un = sn[b]
             for i, (cc, h) in enumerate(chunks):
@@ -386,11 +377,11 @@
 
     plane_loss[p] = lossv[...]
 
-    def l_copy(q, src):
-        slot = plane_loss.at[src]
-        return rcopy(slot, slot, l_send.at[q], l_recv.at[src], (q, j))
-
-    each(1, NP, lambda k: l_copy(nxt(p, k, NP), p).start())
+    def l_start(k):
+        slot = plane_loss.at[p]
+        rcopy(slot, slot, l_send.at[0], l_recv.at[0], (nxt(p, k, NP), j)).start()
+
+    each(1, NP, l_start)
 
     gw_copy.wait_recv()
     for h in range(CB // CH):
@@ -404,12 +395,10 @@
     def gp_copy(k):
         q = nxt(p, k, NP)
         rows = pl.ds(pl.multiple_of(q * DB, DB), DB)
-        return rcopy(gp_all.at[rows], gp_ref.at[:, my_cols], gp_send.at[q], gp_recv.at[p], (q, j))
+        return rcopy(gp_all.at[rows], gp_ref.at[:, my_cols], gp_send.at[0], gp_recv.at[0], (q, j))
 
     def a_sum(xp):
-        for k in range(1, NY):
-            src = nxt(y, k, NY)
-            a_copy(src, xp, src).wait_recv()
+        take(in_a.at[pl.ds(0, NY - 1), pl.ds(2 * xp, 2)], a_recv.at[xp])
         for h in range(2):
             xx = 2 * xp + h
             t = part_a[y, xx]
@@ -422,19 +411,17 @@
                 a2_copy(xx, x).start()
 
     def a2_copy(xx, src):
-        return rcopy(sum_a.at[xx], in_a2.at[src], a2_send.at[xx], a2_recv.at[src], (dp_of(y, xx), j))
+        return rcopy(sum_a.at[xx], in_a2.at[src], a2_send.at[0], a2_recv.at[0], (dp_of(y, xx), j))
 
     def b_sum(yy):
-        for k in range(1, NX):
-            src = nxt(x, k, NX)
-            b_copy(src, yy, src).wait_recv()
+        take(in_b.at[pl.ds(0, NX - 1), yy], b_recv.at[yy])
         t = part_b[x, yy]
         for k in range(1, NX):
             t = t + in_b[nxt(x, k, NX), yy]
         sum_b[yy] = t
 
     def b2_copy(yy, src):
-        return rcopy(sum_b.at[yy], in_b2.at[src], b2_send.at[yy], b2_recv.at[src], (dp_of(yy, x), j))
+        return rcopy(sum_b.at[yy], in_b2.at[src], b2_send.at[0], b2_recv.at[0], (dp_of(yy, x), j))
 
     def b_next(k):
         yy = nxt(y, k, NY)
@@ -448,27 +435,15 @@
     gp_own = pltpu.make_async_copy(gp_all.at[w_rows], gp_ref.at[:, my_cols], own_sem.at[1])
     gp_own.start()
 
-    def l_wait(k):
-        q = nxt(p, k, NP)
-        l_copy(q, q).wait_recv()
-
-    each(1, NP, l_wait)
+    take(plane_loss.at[pl.ds(0, NP - 1)], l_recv.at[0])
     loss_part = plane_loss[0]
     for q in range(1, NP):
         loss_part = loss_part + plane_loss[q]
 
     loss_row = jnp.sum(loss_part, axis=0, keepdims=True)
 
-    def a2_wait(k):
-        src = nxt(x, k, NX)
-        a2_copy(src, src).wait_recv()
-
-    def b2_wait(k):
-        src = nxt(y, k, NY)
-        b2_copy(src, src).wait_recv()
-
-    each(1, NX, a2_wait)
-    each(1, NY, b2_wait)
+    take(in_a2.at[pl.ds(0, NX - 1)], a2_recv.at[0])
+    take(in_b2.at[pl.ds(0, NY - 1)], b2_recv.at[0])
     su, sinv = unit_cols(feats[1, y, x])
     ga, gb = sum_a[x], sum_b[y]
     for k in range(1, NX):
@@ -485,7 +460,7 @@
         msg[q, DB + 3:, :] = jnp.zeros((5, SH), F32)
 
     def m_copy(q, src):
-        return rcopy(msg.at[q], msg_in.at[src], m_send.at[q], m_recv.at[src], (p, q))
+        return rcopy(msg.at[q], msg_in.at[src], m_send.at[0], m_recv.at[0], (p, q))
 
     def m_start(k):
         m_copy(nxt(j, k, NJ), j).start()
@@ -493,11 +468,7 @@
     each(1, NJ, m_start)
     msg_in[j] = msg[j]
 
-    def m_wait(k):
-        src = nxt(j, k, NJ)
-        m_copy(src, src).wait_recv()
-
-    each(1, NJ, m_wait)
+    take(msg_in.at[pl.ds(0, NJ - 1)], m_recv.at[0])
     loss_sum = jnp.zeros((1, SH), F32)
     for h in range(2):
         t = msg_in[h]
@@ -510,36 +481,28 @@
         gs_ref[:, h * SH:(h + 1) * SH] = inv * (t[:DB] - own * dsum)
     loss_ref[0, 0] = -inv_rows * jnp.sum(loss_sum)
 
-    def gp_wait(k):
-        q = nxt(p, k, NP)
-        cols = pl.ds(pl.multiple_of(q * CB, CB), CB)
-        rcopy(gp_all.at[pl.ds(0, DB)], gp_ref.at[:, cols], gp_send.at[q], gp_recv.at[q], (q, j)).wait_recv()
-
-    each(1, NP, gp_wait)
+    take(gp_all.at[pl.ds(0, D - DB)], gp_recv.at[0])
     gp_own.wait()
 
     w_core.wait_send()
     gw_copy.wait_send()
-    for r in range(ITERS):
-        rcopy(core_col.at[r, c], core_col.at[r, c], cc_send.at[r], cc_recv.at[r], peer).wait_send()
-        n = 2 * NP if r == 2 else NP
-        slot = plane_row.at[r, p, pl.ds(0, n)]
-        each(1, NP, lambda k: rcopy(slot, slot, pr_send.at[r, nxt(p, k, NP)], pr_recv.at[r, p], peer).wait_send())
-        zslot = z_row.at[r, z, pl.ds(0, n)]
-        each(1, NZ, lambda k: rcopy(zslot, zslot, zr_send.at[r, nxt(z, k, NZ)], zr_recv.at[r, z], peer).wait_send())
+    for r in range(ITERS + 1):
+        if r < ITERS:
+            take(core_col.at[r, 0], cc_send.at[r])
+        take(plane_row.at[r, pl.ds(0, NP - 1)], pr_send.at[r])
+        take(z_row.at[r, pl.ds(0, NZ - 1)], zr_send.at[r])
     for arr in range(2):
-        each(1, NJ, lambda k: feat_copy(arr, k).wait_send())
+        take(feats.at[arr, 0, 0, pl.ds(0, D - DB)], f_send.at[arr])
         for h in range(2):
-            each(0, NP - 1, lambda n: ag_copy(arr, h, y, x, n, peer).wait_send())
-    each(1, NP, lambda k: w_copy(k).wait_send())
-    each(1, NP, lambda k: gp_copy(k).wait_send())
-    each(1, NP, lambda k: l_copy(nxt(p, k, NP), p).wait_send())
-    each(1, NJ, lambda k: m_copy(nxt(j, k, NJ), j).wait_send())
-    each(1, NX, lambda k: a2_copy(nxt(x, k, NX), x).wait_send())
-    each(1, NY, lambda k: b2_copy(nxt(y, k, NY), y).wait_send())
-    each(1, NY, lambda k: each(0, HX, lambda xp: a_copy(nxt(y, k, NY), xp, y).wait_send()))
-    each(1, NX, lambda k: each(0, NY, lambda yy: b_copy(nxt(x, k, NX), yy, x).wait_send()))
-
+            take(base.at[0, pl.ds(0, ag_rows)], ag_send.at[arr, h])
+    take(wraw.at[0, pl.ds(0, D - DB)], w_send.at[0])
+    take(gp_all.at[pl.ds(0, D - DB)], gp_send.at[0])
+    take(plane_loss.at[pl.ds(0, NP - 1)], l_send.at[0])
+    take(msg_in.at[pl.ds(0, NJ - 1)], m_send.at[0])
+    take(in_a2.at[pl.ds(0, NX - 1)], a2_send.at[0])
+    take(in_b2.at[pl.ds(0, NY - 1)], b2_send.at[0])
+    take(in_a.at[pl.ds(0, NY - 1)], a_send.at[0])
+    take(in_b.at[pl.ds(0, NX - 1)], b_send.at[0])
 
 def body(cfg, teacher_feats, student_feats, prototypes):
     NP, NJ, NY, NX, _, _ = cfg
@@ -557,17 +520,16 @@
         V((2, NY, NX, D, SH), BF16), V((2, D, CB), BF16), V((2, D, CB), BF16), V((2, CB, D), BF16),
         V((NB, D, SB), BF16), V((NB, PC, SB), F32), V((NB, PC, SB), F32), V((PC, SH), F32),
         V((PC, SH), F32), V((NP, SH), F32), V((NP, SH), F32), V((PC, SB), BF16), V((8, SH), F32),
-        V((ITERS, 2, 1, PC), F32), V((ITERS, NP, 2 * NP, SH), F32), V((ITERS, NZ, 2 * NP, SH), F32),
+        V((ITERS, 2, 1, PC), F32), V((ITERS + 1, NP, NP, SH), F32), V((ITERS + 1, NZ, NP, SH), F32),
         V((2, D, CB), F32), V((D, CB), F32), V((D, CB), F32),
         V((NY, NX, DH, SH), F32), V((NX, NY, DH, SH), F32), V((NY, NX, DH, SH), F32), V((NX, NY, DH, SH), F32),
         V((NX, DH, SH), F32), V((NY, DH, SH), F32), V((NX, DH, SH), F32), V((NY, DH, SH), F32),
         V((NJ, DB + 8, SH), F32), V((NJ, DB + 8, SH), F32), V((NP, 8, SH), F32),
-        S((2, NJ)), S((2, NJ)), S((NP,)), S((NP,)), S((2,)),
-        S((4, NP - 1)), S((4, NY, NX)), S((2,)),
-        S((ITERS,)), S((ITERS,)), S((ITERS, NP)), S((ITERS, NP)), S((ITERS, NZ)), S((ITERS, NZ)),
-        S((2,)), S((NP,)), S((NP,)),
-        S((NB,)), S((NB,)), S((NX, NY)), S((NX, NY)), S((NX,)), S((NX,)), S((NY,)), S((NY,)),
-        S((NJ,)), S((NJ,)), S((NP,)), S((NP,)),
+        S((2,)), S((2,)), S((1,)), S((1,)), S((2,)), S((2, 2)), S((2, NY, NX)), S((2, 2)), S((2,)),
+        S((ITERS,)), S((ITERS,)), S((ITERS + 1,)), S((ITERS + 1,)), S((ITERS + 1,)), S((ITERS + 1,)),
+        S((2,)), S((1,)), S((1,)),
+        S((1,)), S((NX // 2,)), S((1,)), S((NY,)), S((1,)), S((1,)), S((1,)), S((1,)),
+        S((1,)), S((1,)), S((1,)), S((1,)),
     ]
     vmem = pl.BlockSpec(memory_space=pltpu.VMEM)
     hbm = pl.BlockSpec(memory_space=pl.ANY)

time: 112 us -> 104 us (0.929)
  Pallas kernels: 106 us -> 98.9 us
    pallas_call x1, Pallas kernels: 106 us -> 98.9 us  [body(): pl.pallas_call(functools.partial(kernel, cfg), out_shape=(jax.ShapeDtypeS...]
where the time goes in v3:
time: 104 us
  Pallas kernels  98.9 us (95%)
  local copies, waits for them, and re-layouts  2.48 us (2%)
  between operations  2.38 us (2%)
    pallas_call x1, Pallas kernels, body(): pl.pallas_call(functools.partial(kernel, cfg), out_shape=(jax.ShapeDtypeS...  98.9 us
    unnamed x4, local copies, waits for them, and re-layouts  2.48 us

profile of v3, /device:TPU:8, one launch (start us, length us, event | category | flops | bytes accessed | tf_op | source)
XLA Modules:
  0.0 103.8 jit_solution(12199531534431962113)
XLA Ops:
  0.6 98.9 %shard_map.58 = (f32[1,1]{1,0:T(1,128)}, f32[16,8192]{1,0:T(8,128)}, f32[16,256]{1,0:T(8,128)}) custom-call(bf16[16,256]{1,0:T(8,128)(2,1)} %bitcast.5, bf16[16,256]{1,0:T(8,128)(2,1)} %bitcast.6, bf16[16,8192]{1,0:T(8,128)(2,1)} %w_ref.1), custom_call_target="tpu_custom_call" | custom-call | tf_op jit(solution)/shard_map/pallas_call | solution.py:536
  100.1 0.0 copy-start
  100.1 1.9 %copy.10 = f32[16,8192]{1,0:T(8,128)} copy(f32[16,8192]{1,0:T(8,128)} %get-tuple-element.13) | data formatting | bytes 1048576
  102.0 0.0 copy-done
  102.0 0.6 copy.11
Async XLA Ops:
  100.1 1.9 %copy-start = (f32[16,256]{1,0:T(8,128)S(1)}, f32[16,256]{1,0:T(8,128)}, u32[]{:S(2)}) copy-start(f32[16,256]{1,0:T(8,128)} %get-tuple-element.8) | copy-start | bytes 49156

commit v4 on v3

--- a/solution.py
+++ b/solution.py
@@ -431,7 +431,6 @@
     each(1, NY, b_next)
     each(0, HX, a_sum)
     b_sum(y)
-    each(1, NP, lambda k: gp_copy(k).start())
     gp_own = pltpu.make_async_copy(gp_all.at[w_rows], gp_ref.at[:, my_cols], own_sem.at[1])
     gp_own.start()
 
@@ -466,6 +465,7 @@
         m_copy(nxt(j, k, NJ), j).start()
 
     each(1, NJ, m_start)
+    each(1, NP, lambda k: gp_copy(k).start())
     msg_in[j] = msg[j]
 
     take(msg_in.at[pl.ds(0, NJ - 1)], m_recv.at[0])
@@ -537,11 +537,11 @@
         functools.partial(kernel, cfg),
         out_shape=(
             jax.ShapeDtypeStruct((1, 1), F32),
-            jax.ShapeDtypeStruct((DB, WC), F32),
-            jax.ShapeDtypeStruct((DB, SB), F32),
+            pltpu.VMEM((DB, WC), F32),
+            pltpu.VMEM((DB, SB), F32),
         ),
         in_specs=[vmem, vmem, hbm],
-        out_specs=(pl.BlockSpec(memory_space=pltpu.SMEM), hbm, vmem),
+        out_specs=(pl.BlockSpec(memory_space=pltpu.SMEM), vmem, vmem),
         scratch_shapes=scratch,
         compiler_params=pltpu.CompilerParams(
             collective_id=0, has_side_effects=True, vmem_limit_bytes=56 * 1024 * 1024

time: 104 us -> 101 us (0.971)
  Pallas kernels: 98.9 us -> 97 us
  local copies, waits for them, and re-layouts: 2.48 us -> 1.4 us
    pallas_call x1, Pallas kernels: 98.9 us -> 97 us  [body(): pl.pallas_call(functools.partial(kernel, cfg), out_shape=(jax.ShapeDtypeS...]
    unnamed x4 -> x2, local copies, waits for them, and re-layouts: 2.48 us -> 1.4 us
where the time goes in v4:
time: 101 us
  Pallas kernels  97 us (96%)
  between operations  2.33 us (2%)
  local copies, waits for them, and re-layouts  1.4 us (1%)
    pallas_call x1, Pallas kernels, body(): pl.pallas_call(functools.partial(kernel, cfg), out_shape=(jax.ShapeDtypeS...  97 us

profile of v4, /device:TPU:8, one launch (start us, length us, event | category | flops | bytes accessed | tf_op | source)
XLA Modules:
  0.0 100.7 jit_solution(436628289204061342)
XLA Ops:
  0.6 97.0 %shard_map.58 = (f32[1,1]{1,0:T(1,128)}, f32[16,8192]{1,0:T(8,128)S(1)}, f32[16,256]{1,0:T(8,128)S(1)}) custom-call(bf16[16,256]{1,0:T(8,128)(2,1)} %bitcast.5, bf16[16,256]{1,0:T(8,128)(2,1)} %bitcast.6, bf16[16,8192]{1,0:T(8,128)(2,1)} %w_ref.1), custom_call_target="tpu_custom_call" | custom-call | tf_op jit(solution)/shard_map/pallas_call | solution.py:536
  97.6 0.8 copy.9
  98.4 0.6 copy.10

commit v5 on v4

--- a/solution.py
+++ b/solution.py
@@ -72,6 +72,20 @@
     def nxt(v, k, n):
         return lax.rem(v + k, n)
 
+    def hops(k, n):
+        return min(k, n - k)
+
+    plane_off = sorted(
+        ((dy, dx) for dy in range(NY) for dx in range(NX) if dy + dx > 0),
+        key=lambda o: -hops(o[0], NY) - hops(o[1], NX))
+    z_off = sorted(range(1, NZ), key=lambda k: -hops(k, NZ))
+
+    def plane_peers():
+        return [dp_of(nxt(y, dy, NY), nxt(x, dx, NX)) for dy, dx in plane_off]
+
+    def proto_peers():
+        return [2 * nxt(z, k, NZ) + cc for k in z_off for cc in (c, oc)] + [2 * z + oc]
+
     barrier = pltpu.get_barrier_semaphore()
 
     def greet_dp(k):
@@ -87,13 +101,13 @@
     my_rows = pl.ds(pl.multiple_of(j * DB, DB), DB)
     my_half = pl.ds(pl.multiple_of(c * SH, SH), SH)
 
-    def feat_copy(arr, k):
-        q = nxt(j, k, NJ)
+    def feat_copy(arr, q):
         lanes = pl.ds(pl.multiple_of(lax.rem(q, 2) * SH, SH), SH)
         src = (t_ref, s_ref)[arr].at[:, lanes]
         return rcopy(src, feats.at[arr, y, x, my_rows], f_send.at[arr], f_recv.at[arr], (p, q))
 
-    each(1, NJ, lambda k: feat_copy(0, k).start())
+    for q in proto_peers():
+        feat_copy(0, q).start()
 
     w_rows = pl.ds(pl.multiple_of(p * DB, DB), DB)
 
@@ -103,7 +117,7 @@
         return rcopy(w_ref.at[:, cols], wraw.at[c, w_rows], w_send.at[0], w_recv.at[0], (q, j))
 
     each(1, NP, lambda k: w_copy(k).start())
-    each(1, NJ, lambda k: feat_copy(1, k).start())
+    each(1, NJ, lambda k: feat_copy(1, nxt(j, k, NJ)).start())
     feats[0, y, x, my_rows, :] = t_ref[:, my_half]
     feats[1, y, x, my_rows, :] = s_ref[:, my_half]
     w_own = pltpu.make_async_copy(
@@ -277,7 +291,8 @@
 
     def plane_start(r):
         slot = plane_row.at[r, p]
-        each(1, NP, lambda k: rcopy(slot, slot, pr_send.at[r], pr_recv.at[r], (nxt(p, k, NP), j)).start())
+        for q in plane_peers():
+            rcopy(slot, slot, pr_send.at[r], pr_recv.at[r], (q, j)).start()
 
     def plane_end(r):
         take(plane_row.at[r, pl.ds(0, NP - 1)], pr_recv.at[r])
@@ -288,7 +303,8 @@
 
     def z_start(r):
         slot = z_row.at[r, z]
-        each(1, NZ, lambda k: rcopy(slot, slot, zr_send.at[r], zr_recv.at[r], (p, 2 * nxt(z, k, NZ) + c)).start())
+        for k in z_off:
+            rcopy(slot, slot, zr_send.at[r], zr_recv.at[r], (p, 2 * nxt(z, k, NZ) + c)).start()
 
     def z_end(r):
         take(z_row.at[r, pl.ds(0, NZ - 1)], zr_recv.at[r])
@@ -461,10 +477,8 @@
     def m_copy(q, src):
         return rcopy(msg.at[q], msg_in.at[src], m_send.at[0], m_recv.at[0], (p, q))
 
-    def m_start(k):
-        m_copy(nxt(j, k, NJ), j).start()
-
-    each(1, NJ, m_start)
+    for q in proto_peers():
+        m_copy(q, j).start()
     each(1, NP, lambda k: gp_copy(k).start())
     msg_in[j] = msg[j]
 

time: 101 us -> 97.8 us (0.968)
  Pallas kernels: 97 us -> 93.8 us
    pallas_call x1, Pallas kernels: 97 us -> 93.8 us  [body(): pl.pallas_call(functools.partial(kernel, cfg), out_shape=(jax.ShapeDtypeS...]
where the time goes in v5:
time: 97.8 us; the launch traced here: 97.5 us
  Pallas kernels  93.8 us (96%)
  between operations  2.33 us (2%)
  local copies, waits for them, and re-layouts  1.4 us (1%)
    pallas_call x1, Pallas kernels, body(): pl.pallas_call(functools.partial(kernel, cfg), out_shape=(jax.ShapeDtypeS...  93.8 us

profile of v5, /device:TPU:8, one launch (start us, length us, event | category | flops | bytes accessed | tf_op | source)
XLA Modules:
  0.0 97.5 jit_solution(13895275602658583668)
XLA Ops:
  0.6 93.8 %shard_map.58 = (f32[1,1]{1,0:T(1,128)}, f32[16,8192]{1,0:T(8,128)S(1)}, f32[16,256]{1,0:T(8,128)S(1)}) custom-call(bf16[16,256]{1,0:T(8,128)(2,1)} %bitcast.5, bf16[16,256]{1,0:T(8,128)(2,1)} %bitcast.6, bf16[16,8192]{1,0:T(8,128)(2,1)} %w_ref.1), custom_call_target="tpu_custom_call" | custom-call | tf_op jit(solution)/shard_map/pallas_call | solution.py:550
  94.5 0.8 copy.9
  95.3 0.6 copy.10

commit v6 on v5

--- a/solution.py
+++ b/solution.py
@@ -42,10 +42,10 @@
     cfg, t_ref, s_ref, w_ref, loss_ref, gp_ref, gs_ref,
     feats, wraw, wn, wtn, sn, base, logit, acc, colb, rscale, tots, gbuf, lossv,
     core_col, plane_row, z_row, gw, gw_in, gp_all,
-    part_a, part_b, in_a, in_b, sum_a, sum_b, in_a2, in_b2, msg, msg_in, plane_loss,
+    part_a, part_b, rel_a, rel_b, in_a, in_b, sum_a, sum_b, in_a2, in_b2, msg, msg_in, plane_loss,
     f_send, f_recv, w_send, w_recv, wc_sem, ag_send, ag_recv, ag_recv_s, own_sem,
     cc_send, cc_recv, pr_send, pr_recv, zr_send, zr_recv, gw_sem, gp_send, gp_recv,
-    a_send, a_recv, b_send, b_recv, a2_send, a2_recv, b2_send, b2_recv,
+    ra_recv, rb_recv, a_send, a_recv, b_send, b_recv, a2_send, a2_recv, b2_send, b2_recv,
     m_send, m_recv, l_send, l_recv,
 ):
     NP, NJ, NY, NX, factor, inv_rows = cfg
@@ -340,15 +340,28 @@
     def row_of(ref, q):
         return jnp.concatenate([ref[pl.ds(q, 1), :], ref[pl.ds(q + 1, 1), :]], axis=1)
 
-    def a_copy(yy, xp):
+    def a_copy(yy, xp, slot):
         xs = pl.ds(2 * xp, 2)
-        return rcopy(part_a.at[yy, xs], in_a.at[y, xs], a_send.at[0], a_recv.at[xp], (dp_of(yy, x), j))
-
-    def b_copy(xx, yy):
-        return rcopy(part_b.at[xx, yy], in_b.at[x, yy], b_send.at[0], b_recv.at[yy], (dp_of(y, xx), j))
+        return rcopy(part_a.at[yy, xs], in_a.at[slot, xs], a_send.at[0], a_recv.at[xp], (dp_of(yy, x), j))
+
+    def a_relay(yy, xp):
+        dev = (dp_of(nxt(y, 1 + 2 * xp, NY), x), j)
+        return rcopy(part_a.at[yy, pl.ds(2 * xp, 2)], rel_a.at[xp], a_send.at[0], ra_recv.at[xp], dev)
+
+    def b_copy(xx, yy, slot):
+        return rcopy(part_b.at[xx, yy], in_b.at[slot, yy], b_send.at[0], b_recv.at[yy], (dp_of(y, xx), j))
+
+    def b_relay(xx, yy, e):
+        dev = (dp_of(y, nxt(x, 1 + 2 * e, NX)), j)
+        return rcopy(part_b.at[xx, yy], rel_b.at[yy], b_send.at[0], rb_recv.at[yy], dev)
+
+    def row_at(k):
+        n = NY - 1 - k
+        return nxt(y, n + n // 2 - 2 * (n // 3), NY)
 
     def grad_rows(k):
-        yy = nxt(y, k + 1, NY)
+        yy = row_at(k)
+        e = lax.rem(yy, 2)
 
         def pair(xp):
             b = yy * HX + xp
@@ -371,14 +384,33 @@
             part_b[2 * xp, yy] = gs[DH:, :SH]
             part_b[2 * xp + 1, yy] = gs[DH:, SH:]
 
-            @pl.when(k < NY - 1)
+            @pl.when(k == 0)
             def _():
-                a_copy(yy, xp).start()
+                a_relay(yy, xp).start()
+
+            @pl.when(k == xp + 1)
+            def _():
+                a_copy(yy, xp, 1 - xp).start()
 
             for h in range(2):
-                @pl.when(2 * xp + h != x)
+                xx = 2 * xp + h
+                d = lax.rem(xx - x + NX, NX)
+
+                @pl.when(jnp.logical_and(k < NY - 1, d == 2))
                 def _():
-                    b_copy(2 * xp + h, yy).start()
+                    b_relay(xx, yy, e).start()
+
+                @pl.when(jnp.logical_and(k == NY - 1, d == 2))
+                def _():
+                    b_copy(xx, yy, 2).start()
+
+                @pl.when(d == 3 - 2 * e)
+                def _():
+                    b_copy(xx, yy, 1 - e).start()
+
+                @pl.when(jnp.logical_and(k == NY - 1, d == 1 + 2 * e))
+                def _():
+                    b_copy(xx, yy, e).start()
 
             un = sn[b]
             for i, (cc, h) in enumerate(chunks):
@@ -390,6 +422,22 @@
 
     gw_copy = rcopy(gw.at[oc], gw_in, gw_sem.at[0], gw_sem.at[1], peer)
     gw_copy.start()
+    for h in range(2):
+        take(rel_a.at[h], ra_recv.at[h])
+        dest = nxt(y, 1 + 2 * h, NY)
+        for i in range(2):
+            part_a[dest, 2 * h + i] += rel_a[h, i]
+        a_copy(dest, h, h).start()
+
+    def b_later(k):
+        yy = row_at(k)
+        e = lax.rem(yy, 2)
+        xx = nxt(x, 1 + 2 * e, NX)
+        take(rel_b.at[yy], rb_recv.at[yy])
+        part_b[xx, yy] += rel_b[yy]
+        b_copy(xx, yy, e).start()
+
+    each(0, NY - 1, b_later)
 
     plane_loss[p] = lossv[...]
 
@@ -414,13 +462,10 @@
         return rcopy(gp_all.at[rows], gp_ref.at[:, my_cols], gp_send.at[0], gp_recv.at[0], (q, j))
 
     def a_sum(xp):
-        take(in_a.at[pl.ds(0, NY - 1), pl.ds(2 * xp, 2)], a_recv.at[xp])
+        take(in_a.at[pl.ds(0, 2), pl.ds(2 * xp, 2)], a_recv.at[xp])
         for h in range(2):
             xx = 2 * xp + h
-            t = part_a[y, xx]
-            for k in range(1, NY):
-                t = t + in_a[nxt(y, k, NY), xx]
-            sum_a[xx] = t
+            sum_a[xx] = part_a[y, xx] + in_a[0, xx] + in_a[1, xx]
 
             @pl.when(xx != x)
             def _():
@@ -429,24 +474,24 @@
     def a2_copy(xx, src):
         return rcopy(sum_a.at[xx], in_a2.at[src], a2_send.at[0], a2_recv.at[0], (dp_of(y, xx), j))
 
-    def b_sum(yy):
-        take(in_b.at[pl.ds(0, NX - 1), yy], b_recv.at[yy])
+    def b_sum(yy, n):
+        take(in_b.at[pl.ds(0, n), yy], b_recv.at[yy])
         t = part_b[x, yy]
-        for k in range(1, NX):
-            t = t + in_b[nxt(x, k, NX), yy]
+        for k in range(n):
+            t = t + in_b[k, yy]
         sum_b[yy] = t
 
     def b2_copy(yy, src):
         return rcopy(sum_b.at[yy], in_b2.at[src], b2_send.at[0], b2_recv.at[0], (dp_of(yy, x), j))
 
     def b_next(k):
-        yy = nxt(y, k, NY)
-        b_sum(yy)
+        yy = row_at(k)
+        b_sum(yy, 2)
         b2_copy(yy, y).start()
 
-    each(1, NY, b_next)
+    each(0, NY - 1, b_next)
     each(0, HX, a_sum)
-    b_sum(y)
+    b_sum(y, 3)
     gp_own = pltpu.make_async_copy(gp_all.at[w_rows], gp_ref.at[:, my_cols], own_sem.at[1])
     gp_own.start()
 
@@ -536,13 +581,14 @@
         V((PC, SH), F32), V((NP, SH), F32), V((NP, SH), F32), V((PC, SB), BF16), V((8, SH), F32),
         V((ITERS, 2, 1, PC), F32), V((ITERS + 1, NP, NP, SH), F32), V((ITERS + 1, NZ, NP, SH), F32),
         V((2, D, CB), F32), V((D, CB), F32), V((D, CB), F32),
-        V((NY, NX, DH, SH), F32), V((NX, NY, DH, SH), F32), V((NY, NX, DH, SH), F32), V((NX, NY, DH, SH), F32),
+        V((NY, NX, DH, SH), F32), V((NX, NY, DH, SH), F32), V((2, 2, DH, SH), F32), V((NY, DH, SH), F32),
+        V((NY, NX, DH, SH), F32), V((NX, NY, DH, SH), F32),
         V((NX, DH, SH), F32), V((NY, DH, SH), F32), V((NX, DH, SH), F32), V((NY, DH, SH), F32),
         V((NJ, DB + 8, SH), F32), V((NJ, DB + 8, SH), F32), V((NP, 8, SH), F32),
         S((2,)), S((2,)), S((1,)), S((1,)), S((2,)), S((2, 2)), S((2, NY, NX)), S((2, 2)), S((2,)),
         S((ITERS,)), S((ITERS,)), S((ITERS + 1,)), S((ITERS + 1,)), S((ITERS + 1,)), S((ITERS + 1,)),
         S((2,)), S((1,)), S((1,)),
-        S((1,)), S((NX // 2,)), S((1,)), S((NY,)), S((1,)), S((1,)), S((1,)), S((1,)),
+        S((2,)), S((NY,)), S((1,)), S((NX // 2,)), S((1,)), S((NY,)), S((1,)), S((1,)), S((1,)), S((1,)),
         S((1,)), S((1,)), S((1,)), S((1,)),
     ]
     vmem = pl.BlockSpec(memory_space=pltpu.VMEM)

time: 97.8 us -> 95.8 us (0.980)
  Pallas kernels: 93.8 us -> 91 us
    pallas_call x1, Pallas kernels: 93.8 us -> 91 us  [body(): pl.pallas_call(functools.partial(kernel, cfg), out_shape=(jax.ShapeDtypeS...]
where the time goes in v6:
time: 95.8 us; the launch traced here: 94.7 us
  Pallas kernels  91 us (95%)
  between operations  2.33 us (2%)
  local copies, waits for them, and re-layouts  1.4 us (1%)
    pallas_call x1, Pallas kernels, body(): pl.pallas_call(functools.partial(kernel, cfg), out_shape=(jax.ShapeDtypeS...  91 us

profile of v6, /device:TPU:8, one launch (start us, length us, event | category | flops | bytes accessed | tf_op | source)
XLA Modules:
  0.0 94.7 jit_solution(14099299675287492767)
XLA Ops:
  0.6 91.0 %shard_map.58 = (f32[1,1]{1,0:T(1,128)}, f32[16,8192]{1,0:T(8,128)S(1)}, f32[16,256]{1,0:T(8,128)S(1)}) custom-call(bf16[16,256]{1,0:T(8,128)(2,1)} %bitcast.5, bf16[16,256]{1,0:T(8,128)(2,1)} %bitcast.6, bf16[16,8192]{1,0:T(8,128)(2,1)} %w_ref.1), custom_call_target="tpu_custom_call" | custom-call | tf_op jit(solution)/shard_map/pallas_call | solution.py:596
  91.6 0.8 copy.9
  92.4 0.6 copy.10

commit v7 on v6

--- a/solution.py
+++ b/solution.py
@@ -39,7 +39,8 @@
 
 
 def kernel(
-    cfg, t_ref, s_ref, w_ref, loss_ref, gp_ref, gs_ref,
+    cfg, t_hbm, s_hbm, w_ref, loss_ref, gp_ref, gs_ref,
+    t_ref, s_ref,
     feats, wraw, wn, wtn, sn, base, logit, acc, colb, rscale, tots, gbuf, lossv,
     core_col, plane_row, z_row, gw, gw_in, gp_all,
     part_a, part_b, rel_a, rel_b, in_a, in_b, sum_a, sum_b, in_a2, in_b2, msg, msg_in, plane_loss,
@@ -96,7 +97,13 @@
 
     each(1, NP, greet_dp)
     each(1, NJ, greet_proto)
+    t_in = pltpu.make_async_copy(t_hbm, t_ref, own_sem.at[2])
+    s_in = pltpu.make_async_copy(s_hbm, s_ref, own_sem.at[3])
+    t_in.start()
+    s_in.start()
     pl.semaphore_wait(barrier, NP + NJ - 2)
+    t_in.wait()
+    s_in.wait()
 
     my_rows = pl.ds(pl.multiple_of(j * DB, DB), DB)
     my_half = pl.ds(pl.multiple_of(c * SH, SH), SH)
@@ -314,9 +321,6 @@
         return total
 
     for r in range(ITERS):
-        if r == 2:
-            plane_end(ITERS)
-            z_start(ITERS)
         if r > 0:
             col_pass()
         col_exchange(r)
@@ -328,9 +332,13 @@
             for h in range(2):
                 take(feats.at[1, pl.ds(0, NY - 1), :, pl.ds(0, DH)], ag_recv_s.at[h, 1])
             each(0, NY, student_rows)
-            plane_start(ITERS)
+        if r == 2:
+            plane_end(ITERS)
+            z_start(ITERS)
         plane_end(r)
         z_start(r)
+        if r == 1:
+            plane_start(ITERS)
         rscale[...] = 1.0 / z_end(r)
     tots[...] = z_end(ITERS)
 
@@ -502,9 +510,13 @@
 
     loss_row = jnp.sum(loss_part, axis=0, keepdims=True)
 
+    su, sinv = unit_cols(feats[1, y, x])
+    for q in range(NJ):
+        msg[q, DB + 1:DB + 2, :] = sinv
+        msg[q, DB + 2:DB + 3, :] = loss_row
+        msg[q, DB + 3:, :] = jnp.zeros((5, SH), F32)
     take(in_a2.at[pl.ds(0, NX - 1)], a2_recv.at[0])
     take(in_b2.at[pl.ds(0, NY - 1)], b2_recv.at[0])
-    su, sinv = unit_cols(feats[1, y, x])
     ga, gb = sum_a[x], sum_b[y]
     for k in range(1, NX):
         ga = ga + in_a2[nxt(x, k, NX)]
@@ -515,9 +527,6 @@
         lo = q * DB
         msg[q, :DB, :] = ga[lo:lo + DB] if lo < DH else gb[lo - DH:lo - DH + DB]
         msg[q, DB:DB + 1, :] = dots
-        msg[q, DB + 1:DB + 2, :] = sinv
-        msg[q, DB + 2:DB + 3, :] = loss_row
-        msg[q, DB + 3:, :] = jnp.zeros((5, SH), F32)
 
     def m_copy(q, src):
         return rcopy(msg.at[q], msg_in.at[src], m_send.at[0], m_recv.at[0], (p, q))
@@ -576,6 +585,7 @@
     NB = NP // 2
     V, S = pltpu.VMEM, pltpu.SemaphoreType.DMA
     scratch = [
+        V((DB, SB), BF16), V((DB, SB), BF16),
         V((2, NY, NX, D, SH), BF16), V((2, D, CB), BF16), V((2, D, CB), BF16), V((2, CB, D), BF16),
         V((NB, D, SB), BF16), V((NB, PC, SB), F32), V((NB, PC, SB), F32), V((PC, SH), F32),
         V((PC, SH), F32), V((NP, SH), F32), V((NP, SH), F32), V((PC, SB), BF16), V((8, SH), F32),
@@ -585,7 +595,7 @@
         V((NY, NX, DH, SH), F32), V((NX, NY, DH, SH), F32),
         V((NX, DH, SH), F32), V((NY, DH, SH), F32), V((NX, DH, SH), F32), V((NY, DH, SH), F32),
         V((NJ, DB + 8, SH), F32), V((NJ, DB + 8, SH), F32), V((NP, 8, SH), F32),
-        S((2,)), S((2,)), S((1,)), S((1,)), S((2,)), S((2, 2)), S((2, NY, NX)), S((2, 2)), S((2,)),
+        S((2,)), S((2,)), S((1,)), S((1,)), S((2,)), S((2, 2)), S((2, NY, NX)), S((2, 2)), S((4,)),
         S((ITERS,)), S((ITERS,)), S((ITERS + 1,)), S((ITERS + 1,)), S((ITERS + 1,)), S((ITERS + 1,)),
         S((2,)), S((1,)), S((1,)),
         S((2,)), S((NY,)), S((1,)), S((NX // 2,)), S((1,)), S((NY,)), S((1,)), S((1,)), S((1,)), S((1,)),
@@ -600,7 +610,7 @@
             pltpu.VMEM((DB, WC), F32),
             pltpu.VMEM((DB, SB), F32),
         ),
-        in_specs=[vmem, vmem, hbm],
+        in_specs=[hbm, hbm, hbm],
         out_specs=(pl.BlockSpec(memory_space=pltpu.SMEM), vmem, vmem),
         scratch_shapes=scratch,
         compiler_params=pltpu.CompilerParams(

time: 95.8 us -> 95.2 us (level)
  Pallas kernels: 91 us -> 90 us
where the time goes in v7:
time: 95.2 us; the launch traced here: 93.8 us
  Pallas kernels  90 us (95%)
  between operations  2.33 us (2%)
  local copies, waits for them, and re-layouts  1.4 us (1%)
    pallas_call x1, Pallas kernels, body(): pl.pallas_call(functools.partial(kernel, cfg), out_shape=(jax.ShapeDtypeS...  90 us

profile of v7, /device:TPU:8, one launch (start us, length us, event | category | flops | bytes accessed | tf_op | source)
XLA Modules:
  0.0 93.8 jit_solution(8393732322821016879)
XLA Ops:
  0.6 90.0 %shard_map.58 = (f32[1,1]{1,0:T(1,128)}, f32[16,8192]{1,0:T(8,128)S(1)}, f32[16,256]{1,0:T(8,128)S(1)}) custom-call(bf16[16,256]{1,0:T(8,128)(2,1)} %bitcast.5, bf16[16,256]{1,0:T(8,128)(2,1)} %bitcast.6, bf16[16,8192]{1,0:T(8,128)(2,1)} %w_ref.1), custom_call_target="tpu_custom_call" | custom-call | tf_op jit(solution)/shard_map/pallas_call | solution.py:606
  90.7 0.8 copy.9
  91.5 0.6 copy.10

commit v8 on v7

--- a/solution.py
+++ b/solution.py
@@ -193,8 +193,6 @@
     w_core = rcopy(wraw.at[c], wraw.at[c], wc_sem.at[0], wc_sem.at[1], peer)
     w_core.start()
     forward(0)
-    feat_wait(1)
-    own_out(1)
 
     def unit_cols(v):
         v32 = v.astype(F32)
@@ -236,6 +234,8 @@
         each(0, HX, pair)
 
     each(0, NY, teacher_rows)
+    feat_wait(1)
+    own_out(1)
 
     def student_rows(yy):
 
@@ -326,8 +326,6 @@
         col_exchange(r)
         row_pass(r)
         plane_start(r)
-        if r == 0:
-            forward(1)
         if r == 1:
             for h in range(2):
                 take(feats.at[1, pl.ds(0, NY - 1), :, pl.ds(0, DH)], ag_recv_s.at[h, 1])
@@ -337,6 +335,8 @@
             z_start(ITERS)
         plane_end(r)
         z_start(r)
+        if r == 0:
+            forward(1)
         if r == 1:
             plane_start(ITERS)
         rscale[...] = 1.0 / z_end(r)

time: 95.2 us -> 94.9 us (level)
  no operation moved by 1% of the time
where the time goes in v8:
time: 94.9 us; the launch traced here: 93.8 us
  Pallas kernels  90.1 us (95%)
  between operations  2.33 us (2%)
  local copies, waits for them, and re-layouts  1.4 us (1%)
    pallas_call x1, Pallas kernels, body(): pl.pallas_call(functools.partial(kernel, cfg), out_shape=(jax.ShapeDtypeS...  90.1 us

profile of v8, /device:TPU:8, one launch (start us, length us, event | category | flops | bytes accessed | tf_op | source)
XLA Modules:
  0.0 93.8 jit_solution(4926498014333128002)
XLA Ops:
  0.6 90.1 %shard_map.58 = (f32[1,1]{1,0:T(1,128)}, f32[16,8192]{1,0:T(8,128)S(1)}, f32[16,256]{1,0:T(8,128)S(1)}) custom-call(bf16[16,256]{1,0:T(8,128)(2,1)} %bitcast.5, bf16[16,256]{1,0:T(8,128)(2,1)} %bitcast.6, bf16[16,8192]{1,0:T(8,128)(2,1)} %w_ref.1), custom_call_target="tpu_custom_call" | custom-call | tf_op jit(solution)/shard_map/pallas_call | solution.py:606
  90.7 0.8 copy.9
  91.5 0.6 copy.10

commit v9 on v8

--- a/solution.py
+++ b/solution.py
@@ -124,7 +124,6 @@
         return rcopy(w_ref.at[:, cols], wraw.at[c, w_rows], w_send.at[0], w_recv.at[0], (q, j))
 
     each(1, NP, lambda k: w_copy(k).start())
-    each(1, NJ, lambda k: feat_copy(1, nxt(j, k, NJ)).start())
     feats[0, y, x, my_rows, :] = t_ref[:, my_half]
     feats[1, y, x, my_rows, :] = s_ref[:, my_half]
     w_own = pltpu.make_async_copy(
@@ -187,6 +186,7 @@
 
     feat_wait(0)
     own_out(0)
+    each(1, NJ, lambda k: feat_copy(1, nxt(j, k, NJ)).start())
 
     take(wraw.at[c, pl.ds(0, D - DB)], w_recv.at[0])
     w_own.wait()

time: 94.9 us -> 94.3 us (level)
  no operation moved by 1% of the time
where the time goes in v9:
time: 94.3 us; the launch traced here: 93.2 us
  Pallas kernels  89.5 us (95%)
  between operations  2.33 us (2%)
  local copies, waits for them, and re-layouts  1.4 us (1%)
    pallas_call x1, Pallas kernels, body(): pl.pallas_call(functools.partial(kernel, cfg), out_shape=(jax.ShapeDtypeS...  89.5 us

profile of v9, /device:TPU:8, one launch (start us, length us, event | category | flops | bytes accessed | tf_op | source)
XLA Modules:
  0.0 93.2 jit_solution(12295962976641794567)
XLA Ops:
  0.6 89.5 %shard_map.58 = (f32[1,1]{1,0:T(1,128)}, f32[16,8192]{1,0:T(8,128)S(1)}, f32[16,256]{1,0:T(8,128)S(1)}) custom-call(bf16[16,256]{1,0:T(8,128)(2,1)} %bitcast.5, bf16[16,256]{1,0:T(8,128)(2,1)} %bitcast.6, bf16[16,8192]{1,0:T(8,128)(2,1)} %w_ref.1), custom_call_target="tpu_custom_call" | custom-call | tf_op jit(solution)/shard_map/pallas_call | solution.py:606
  90.1 0.8 copy.9
  90.9 0.6 copy.10

commit v10 on v8

--- a/solution.py
+++ b/solution.py
@@ -445,7 +445,8 @@
         part_b[xx, yy] += rel_b[yy]
         b_copy(xx, yy, e).start()
 
-    each(0, NY - 1, b_later)
+    for k in range(NY - 1):
+        b_later(k)
 
     plane_loss[p] = lossv[...]
 
@@ -497,8 +498,10 @@
         b_sum(yy, 2)
         b2_copy(yy, y).start()
 
-    each(0, NY - 1, b_next)
-    each(0, HX, a_sum)
+    for k in range(NY - 1):
+        b_next(k)
+    for xp in range(HX):
+        a_sum(xp)
     b_sum(y, 3)
     gp_own = pltpu.make_async_copy(gp_all.at[w_rows], gp_ref.at[:, my_cols], own_sem.at[1])
     gp_own.start()

time: 94.9 us -> 94.9 us (level)
  no operation moved by 1% of the time
where the time goes in v10:
time: 94.9 us; the launch traced here: 93.8 us
  Pallas kernels  90.1 us (95%)
  between operations  2.33 us (2%)
  local copies, waits for them, and re-layouts  1.4 us (1%)
    pallas_call x1, Pallas kernels, body(): pl.pallas_call(functools.partial(kernel, cfg), out_shape=(jax.ShapeDtypeS...  90.1 us

profile of v10, /device:TPU:8, one launch (start us, length us, event | category | flops | bytes accessed | tf_op | source)
XLA Modules:
  0.0 93.8 jit_solution(18321946597709906942)
XLA Ops:
  0.6 90.1 %shard_map.58 = (f32[1,1]{1,0:T(1,128)}, f32[16,8192]{1,0:T(8,128)S(1)}, f32[16,256]{1,0:T(8,128)S(1)}) custom-call(bf16[16,256]{1,0:T(8,128)(2,1)} %bitcast.5, bf16[16,256]{1,0:T(8,128)(2,1)} %bitcast.6, bf16[16,8192]{1,0:T(8,128)(2,1)} %w_ref.1), custom_call_target="tpu_custom_call" | custom-call | tf_op jit(solution)/shard_map/pallas_call | solution.py:609
  90.7 0.8 copy.9
  91.5 0.6 copy.10
